TPU v7x, 128 devices: a whole 4x4x4 slice. The times are simulated.
128 devices in a mesh: dp: 8 (over z, core), mp: 16 (over y, x).
Axes of the slice: x: 4, y: 4, z: 4, core: 2. Of those that a mesh axis runs over, the one named last changes fastest.
Arguments:
- grads: bfloat16 [128, 512, 512], P(None, ('dp', 'mp')), may hold values from -150 to 150
- block_slot: int32 [128], replicated, may hold values from 0 to 255, as said below
- iters_count: int32 [128], replicated, may hold values from 2 to 3
- stat_left: float32 [256, 512, 512], P(('dp', 'mp')), may hold values from -3 to 303, as said below
- stat_right: float32 [256, 512, 512], P(('dp', 'mp')), may hold values from -3 to 303, as said below
Outputs:
- update: float32 [128, 512, 512], P(None, ('dp', 'mp'))
- new_left: float32 [256, 512, 512], P(('dp', 'mp'))
- new_right: float32 [256, 512, 512], P(('dp', 'mp'))
Inputs may be any that keep to these rules, and one draw needn't show every extreme that they name: `block_slot`: the 128 values are distinct. Slot s is position s % 2 of the device whose flattened index, dp index times the size of mp plus mp index, is s // 2. Some device owns 2 blocks. `stat_left`: each slot holds a symmetric positive definite matrix. `stat_right`: each slot holds a symmetric positive definite matrix.
All inputs are finite; a program needn't handle non-finite values.
Results may differ from a plain program's by a relative error of at most 0.0003.
Values may be sent and summed in bfloat16 or wider, within the bound.
A program may use at most 64 MiB of HBM per device.

v0:
```python
import math

import jax
import jax.numpy as jnp
from jax import lax
from jax.sharding import PartitionSpec as P

ITERS = 3


STAT_DECAY = 0.95
CLIP_SHARE = 0.5
EPSILON = 1e-06


def batched(former, latter):
    return jnp.matmul(former, latter, precision=lax.Precision.HIGHEST)


def inverse_roots(stacked, counts):
    block_size = stacked.shape[-1]
    identity = jnp.eye(block_size, dtype=jnp.float32)
    frobenius = jnp.sqrt(jnp.sum(stacked * stacked, axis=(1, 2), keepdims=True))
    moment = stacked / frobenius
    estimate = jnp.broadcast_to(identity, stacked.shape)
    for iteration in range(ITERS):
        active = (iteration < counts)[:, None, None]
        factor = (5.0 * identity - moment) * 0.25
        estimate = jnp.where(active, batched(estimate, factor), estimate)
        if iteration < ITERS - 1:
            square = batched(factor, factor)
            fourth = batched(square, square)
            moment = jnp.where(active, batched(fourth, moment), moment)
    return estimate


def refresh_blocks(blocks, left_stats, right_stats, counts, clipping):
    gram_rows = jnp.einsum("nij,nkj->nik", blocks, blocks, preferred_element_type=jnp.float32)
    gram_cols = jnp.einsum("nji,njk->nik", blocks, blocks, preferred_element_type=jnp.float32)
    squared = clipping * clipping
    fresh_left = STAT_DECAY * left_stats + squared * gram_rows
    fresh_right = STAT_DECAY * right_stats + squared * gram_cols
    members = blocks.shape[0]
    inverse_root = inverse_roots(
        jnp.concatenate([fresh_left, fresh_right], axis=0),
        jnp.concatenate([counts, counts], axis=0),
    )
    widened = blocks.astype(jnp.float32)
    product = batched(batched(inverse_root[:members], widened), inverse_root[members:])
    grad_norm = jnp.sqrt(jnp.sum(widened * widened, axis=(1, 2), keepdims=True))
    prod_norm = jnp.sqrt(jnp.sum(product * product, axis=(1, 2), keepdims=True))
    result = clipping * grad_norm * product / (prod_norm + EPSILON)
    return (fresh_left, fresh_right, result)


def per_device(grads, block_slot, iters_count, stat_left, stat_right):
    dp_size = lax.axis_size("dp")
    mp_size = lax.axis_size("mp")
    devices = dp_size * mp_size
    myself = lax.axis_index("dp") * mp_size + lax.axis_index("mp")
    blocks_all, row_share, block_size = grads.shape
    capacity = stat_left.shape[0]
    widened_rows = grads.astype(jnp.float32)
    square_sum = lax.psum(jnp.sum(widened_rows * widened_rows), ("dp", "mp"))
    clipping = jnp.minimum(
        1.0, CLIP_SHARE * block_size * math.sqrt(blocks_all) / (jnp.sqrt(square_sum) + EPSILON)
    )
    owner_of = block_slot // capacity
    place_of = block_slot % capacity
    target = place_of * devices + owner_of
    selector = (target[None, :] == jnp.arange(capacity * devices, dtype=jnp.int32)[:, None]).astype(
        jnp.bfloat16
    )
    outgoing = jnp.dot(
        selector,
        grads.reshape(blocks_all, row_share * block_size),
        preferred_element_type=jnp.float32,
    )
    outgoing = outgoing.astype(jnp.bfloat16).reshape(capacity, devices, row_share, block_size)
    arrived = lax.all_to_all(outgoing, ("dp", "mp"), split_axis=1, concat_axis=1, tiled=True)
    owned_blocks = arrived.reshape(capacity, block_size, block_size)
    my_slots = myself * capacity + jnp.arange(capacity, dtype=jnp.int32)
    matches = block_slot[None, :] == my_slots[:, None]
    is_live = jnp.any(matches, axis=1)[:, None, None]
    counts = jnp.sum(jnp.where(matches, iters_count[None, :], 0), axis=1)
    fresh_left, fresh_right, result = refresh_blocks(
        owned_blocks, stat_left, stat_right, counts, clipping
    )
    new_left = jnp.where(is_live, fresh_left, stat_left)
    new_right = jnp.where(is_live, fresh_right, stat_right)
    leaving = result.reshape(capacity, devices, row_share, block_size)
    returned = lax.all_to_all(leaving, ("dp", "mp"), split_axis=1, concat_axis=1, tiled=True)
    flat_rows = returned.reshape(capacity * devices, row_share * block_size)
    update_rows = jnp.take(flat_rows, target, axis=0).reshape(blocks_all, row_share, block_size)
    return (update_rows, new_left, new_right)


def solution(mesh):
    in_specs = (
        P(None, ("dp", "mp"), None),
        P(),
        P(),
        P(("dp", "mp"), None, None),
        P(("dp", "mp"), None, None),
    )
    out_specs = (
        P(None, ("dp", "mp"), None),
        P(("dp", "mp"), None, None),
        P(("dp", "mp"), None, None),
    )
    return jax.shard_map(
        per_device, mesh=mesh, in_specs=in_specs, out_specs=out_specs, check_vma=False
    )
```

profile of v0, /device:TPU:1, one launch (start us, length us, event | category | flops | bytes accessed | tf_op | source)
XLA Modules:
  0.0 221.4 jit_solution(12188267342165238122)
XLA Ops:
  0.6 0.7 compare_and_fusion
  1.3 1.1 copy.20
  2.9 0.8 reshape.111
  3.7 1.3 copy.14
  5.1 11.5 %all-to-all-start = ((bf16[2,128,4,512]{3,2,0,1:T(4,128)(2,1)}), bf16[2,128,4,512]{3,2,0,1:T(4,128)(2,1)S(1)}, u32[]{:S(2)}, u32[]{:S(2)}) async-start(bf16[2,128,4,512]{3,2,0,1:T(4,128)(2,1)} %copy.14), calls=%async_computation | async-start | bytes 2097152 | tf_op jit(solution)/shard_map/all_to_all | solution.py:80
  16.6 1.1 multiply_reduce_fusion.3
  17.7 69.3 %psum.7 = f32[]{:T(128)} all-reduce(f32[]{:T(128)} %multiply_reduce_fusion.3), channel_id=1, replica_groups=mesh['dp'=8,'mp'=16] {'dp','mp'}, use_global_device_ids=true, to_apply=%region_1.0 | all-reduce | flops 1 | bytes 8 | tf_op jit(solution)/shard_map/psum | solution.py:64
  88.4 1.1 fusion.32
  89.5 1.3 copy.15
  90.8 1.9 reshape.112
  92.7 2.5 %multiply_add_fusion.1 = f32[2,512,512]{2,1,0:T(8,128)S(1)} fusion(f32[2,512,512]{2,1,0:T(8,128)} %param.8, bf16[2,512,512]{2,1,0:T(8,128)(2,1)S(1)} %reshape.112, f32[]{:T(128)S(6)} %mul.92), kind=kOutput, calls=%fused_computation.29 | convolution fusion | flops 538443776 | bytes 5242884 | tf_op jit(solution)/shard_map/nij,nkj->nik/dot_general | solution.py:38
  95.5 3.0 %broadcast_select_fusion = (f32[2,512,512]{2,1,0:T(8,128)}, f32[2,512,512]{2,1,0:T(8,128)}, f32[2,512,512]{2,1,0:T(8,128)S(1)}) fusion(f32[2,512,512]{2,1,0:T(8,128)S(1)} %copy-done.4, pred[2]{0:T(512)(128)(4,1)S(1)} %compare_reduce_fusion, f32[2,512,512]{2,1,0:T(8,128)S(1)} %multiply_add_fusion.1, f32[2,512,512]{2,1,0:T(8,128)S(1)} %copy-done, ...), kind=kOutput, calls=%fused_computation.44 | convolution fusion | flops 539492352 | bytes 13631494 | tf_op jit(solution)/shard_map/nji,njk->nik/dot_general | solution.py:39
  99.0 8.1 %fusion.6 = f32[4,512,512]{2,1,0:T(8,128)S(1)} fusion(f32[512,512]{1,0:T(8,128)S(1)} %fusion.31, f32[2,512,512]{2,1,0:T(8,128)S(1)} %get-tuple-element.12, f32[2,512,512]{2,1,0:T(8,128)S(1)} %multiply_add_fusion.1, f32[4]{0:T(128)S(1)} %sqrt.29), kind=kOutput, calls=%fused_computation.12 | convolution fusion | flops 6446645248 | bytes 9437200 | tf_op jit(solution)/shard_map/dot_general | solution.py:17
  107.1 7.3 %fusion.46 = f32[4,512,512]{2,1,0:T(8,128)S(1)} fusion(f32[4,512,512]{2,1,0:T(8,128)S(1)} %fusion.6), kind=kOutput, calls=%fused_computation.74 | convolution fusion | flops 6442450944 | bytes 8388608 | tf_op jit(solution)/shard_map/dot_general | solution.py:17
  114.4 9.5 %fusion.7 = f32[4,512,512]{2,1,0:T(8,128)} fusion(f32[512,512]{1,0:T(8,128)S(1)} %fusion.31, f32[512,512]{1,0:T(8,128)S(1)} %copy-done.2, f32[2,512,512]{2,1,0:T(8,128)S(1)} %get-tuple-element.12, f32[2,512,512]{2,1,0:T(8,128)S(1)} %multiply_add_fusion.1, f32[4]{0:T(128)S(1)} %sqrt.29), kind=kOutput, calls=%fused_computation.13 | convolution fusion | flops 6446645248 | bytes 10485776 | tf_op jit(solution)/shard_map/dot_general | solution.py:17
  123.8 7.4 %convolution_select_fusion = f32[4,512,512]{2,1,0:T(8,128)S(1)} fusion(f32[4,512,512]{2,1,0:T(8,128)S(1)} %fusion.46, pred[4]{0:T(512)(128)(4,1)S(1)} %get-tuple-element.9, f32[4]{0:T(128)S(1)} %sqrt.29, f32[2,512,512]{2,1,0:T(8,128)S(1)} %get-tuple-element.12, f32[2,512,512]{2,1,0:T(8,128)S(1)} %multiply_add_fusion.1), kind=kOutput, calls=%fused_computation.16 | convolution fusion | flops 6447693824 | bytes 12582932 | tf_op jit(solution)/shard_map/dot_general | solution.py:17
  131.3 8.0 %fusion.8 = f32[4,512,512]{2,1,0:T(8,128)S(1)} fusion(f32[4,512,512]{2,1,0:T(8,128)S(1)} %convolution_select_fusion, f32[512,512]{1,0:T(8,128)S(1)} %fusion.31), kind=kOutput, calls=%fused_computation.14 | convolution fusion | flops 6444548096 | bytes 9437184 | tf_op jit(solution)/shard_map/dot_general | solution.py:17
  139.3 7.1 %fusion.47 = f32[4,512,512]{2,1,0:T(8,128)S(1)} fusion(f32[4,512,512]{2,1,0:T(8,128)S(1)} %fusion.8), kind=kOutput, calls=%fused_computation.75 | convolution fusion | flops 6442450944 | bytes 8388608 | tf_op jit(solution)/shard_map/dot_general | solution.py:17
  146.4 7.2 %fusion.48 = f32[4,512,512]{2,1,0:T(8,128)S(1)} fusion(f32[4,512,512]{2,1,0:T(8,128)S(1)} %fusion.47, f32[4,512,512]{2,1,0:T(8,128)S(1)} %convolution_select_fusion), kind=kOutput, calls=%fused_computation.76 | convolution fusion | flops 6442450944 | bytes 12582912 | tf_op jit(solution)/shard_map/dot_general | solution.py:17
  153.6 7.4 %select_select_fusion = f32[4,512,512]{2,1,0:T(8,128)S(1)} fusion(f32[4,512,512]{2,1,0:T(8,128)S(1)} %copy-done.1, f32[4,512,512]{2,1,0:T(8,128)S(1)} %convolution_select_fusion, f32[512,512]{1,0:T(8,128)S(1)} %fusion.31, f32[512,512]{1,0:T(8,128)S(1)} %copy-done.2, pred[4]{0:T(512)(128)(4,1)S(1)} %get-tuple-element.9, pred[4]{0:T(512)(128)(4,1)S(1)} %get-tuple-element.8), kind=kOutput, calls=%fused_computation.9 | convolution fusion | flops 6447693824 | bytes 14680072 | tf_op jit(solution)/shard_map/dot_general | solution.py:17
  161.1 7.8 %fusion.12 = f32[4,512,512]{2,1,0:T(8,128)S(1)} fusion(f32[4,512,512]{2,1,0:T(8,128)S(1)} %select_select_fusion, f32[4,512,512]{2,1,0:T(8,128)S(1)} %fusion.48, f32[4,512,512]{2,1,0:T(8,128)S(1)} %convolution_select_fusion, f32[512,512]{1,0:T(8,128)S(1)} %fusion.31, pred[4]{0:T(512)(128)(4,1)S(1)} %get-tuple-element.8, pred[4]{0:T(512)(128)(4,1)S(1)} %get-tuple-element.7), kind=kOutput, calls=%fused_computation.18 | convolution fusion | flops 6446645248 | bytes 17825800 | tf_op jit(solution)/shard_map/dot_general | solution.py:17
  168.9 1.9 fusion.49
  170.8 3.8 %multiply_reduce_fusion.1 = (f32[2]{0:T(128)S(1)}, f32[2,512,512]{2,1,0:T(8,128)S(1)}) fusion(f32[2,512,512]{2,1,0:T(8,128)S(1)} %fusion.49, f32[4,512,512]{2,1,0:T(8,128)S(1)} %fusion.12), kind=kOutput, calls=%fused_computation.21 | convolution fusion | flops 3222274048 | bytes 6291464 | tf_op jit(solution)/shard_map/dot_general | solution.py:17
  174.5 0.7 multiply_reduce_fusion.2
  175.6 1.7 reshape.113
  177.3 3.6 %copy.17 = f32[2,128,4,512]{3,2,0,1:T(4,128)} copy(f32[2,128,4,512]{3,2,1,0:T(4,128)} %reshape.113) | data formatting | bytes 4194304 | tf_op jit(solution)/shard_map/reshape | solution.py:91
  180.9 6.4 %all-to-all-start.1 = ((f32[2,128,4,512]{3,2,0,1:T(4,128)}), f32[2,128,4,512]{3,2,0,1:T(4,128)S(1)}, u32[]{:S(2)}, u32[]{:S(2)}) async-start(f32[2,128,4,512]{3,2,0,1:T(4,128)} %copy.17), calls=%async_computation.1 | async-start | bytes 4194304 | tf_op jit(solution)/shard_map/all_to_all | solution.py:92
  187.3 29.6 %all-to-all-done.1 = f32[2,128,4,512]{3,2,0,1:T(4,128)S(1)} async-done(((f32[2,128,4,512]{3,2,0,1:T(4,128)}), f32[2,128,4,512]{3,2,0,1:T(4,128)S(1)}, u32[]{:S(2)}, u32[]{:S(2)}) %all-to-all-start.1) | async-done | bytes 2097184 | tf_op jit(solution)/shard_map/all_to_all | solution.py:92
  217.2 0.9 copy.21
  218.1 1.0 gather_fusion
  219.1 0.7 gather.7
  219.8 1.3 broadcast_select_fusion.2
  (28 shorter events, 2.6 us)
Async XLA Ops:
  2.5 14.1 %copy-start.3 = (bf16[128,4,512]{2,1,0:T(4,128)(2,1)S(1)}, bf16[128,4,512]{2,1,0:T(4,128)(2,1)}, u32[]{:S(2)}) copy-start(bf16[128,4,512]{2,1,0:T(4,128)(2,1)} %param.5) | copy-start | bytes 1572868
  2.5 85.3 %copy-start.5 = (s32[128]{0:T(128)S(1)}, s32[128]{0:T(128)}, u32[]{:S(2)}) copy-start(s32[128]{0:T(128)} %param.7) | copy-start | bytes 1540
  2.5 85.3 %copy-start.6 = (s32[128]{0:T(128)S(1)}, s32[128]{0:T(128)}, u32[]{:S(2)}) copy-start(s32[128]{0:T(128)} %param.6) | copy-start | bytes 1540
  5.1 84.4 %all-to-all-start = ((bf16[2,128,4,512]{3,2,0,1:T(4,128)(2,1)}), bf16[2,128,4,512]{3,2,0,1:T(4,128)(2,1)S(1)}, u32[]{:S(2)}, u32[]{:S(2)}) async-start(bf16[2,128,4,512]{3,2,0,1:T(4,128)(2,1)} %copy.14), calls=%async_computation | async-start | bytes 2097152 | tf_op jit(solution)/shard_map/all_to_all | solution.py:80
  92.7 2.5 %copy-start = (f32[2,512,512]{2,1,0:T(8,128)S(1)}, f32[2,512,512]{2,1,0:T(8,128)}, u32[]{:S(2)}) copy-start(f32[2,512,512]{2,1,0:T(8,128)} %param.8) | copy-start | bytes 6291460
  92.7 2.8 %copy-start.4 = (f32[2,512,512]{2,1,0:T(8,128)S(1)}, f32[2,512,512]{2,1,0:T(8,128)}, u32[]{:S(2)}) copy-start(f32[2,512,512]{2,1,0:T(8,128)} %param.9) | copy-start | bytes 6291460
  107.1 7.3 %copy-start.2 = (f32[512,512]{1,0:T(8,128)S(1)}, f32[512,512]{1,0:T(8,128)}, u32[]{:S(2)}) copy-start(f32[512,512]{1,0:T(8,128)} %fusion.32) | copy-start | bytes 3145732
  146.4 7.2 %copy-start.1 = (f32[4,512,512]{2,1,0:T(8,128)S(1)}, f32[4,512,512]{2,1,0:T(8,128)}, u32[]{:S(2)}) copy-start(f32[4,512,512]{2,1,0:T(8,128)} %fusion.7) | copy-start | bytes 12582916
  180.9 36.0 %all-to-all-start.1 = ((f32[2,128,4,512]{3,2,0,1:T(4,128)}), f32[2,128,4,512]{3,2,0,1:T(4,128)S(1)}, u32[]{:S(2)}, u32[]{:S(2)}) async-start(f32[2,128,4,512]{3,2,0,1:T(4,128)} %copy.17), calls=%async_computation.1 | async-start | bytes 4194304 | tf_op jit(solution)/shard_map/all_to_all | solution.py:92
where the time goes:
time: 226 us; the launch traced here: 221 us
  matrix products  81.3 us (36%)
  blocking collectives  69.3 us (31%)
  waiting for transfers between devices  29.6 us (13%)
  starting transfers between devices  17.9 us (8%)
  local copies, waits for them, and re-layouts  15.1 us (7%)
  other arithmetic  6.29 us (3%)
    dot_general x11, matrix products, batched(): return jnp.matmul(former, latter, precision=lax.Precision.HIGHEST)  75.4 us
    psum x1, blocking collectives, per_device(): square_sum = lax.psum(jnp.sum(widened_rows * widened_rows), ('dp', 'mp'))  69.3 us
    all_to_all x1, waiting for transfers between devices, per_device(): lax.all_to_all(leaving, ('dp', 'mp'), split_axis=1, concat_axis=1, tiled=...  29.6 us
    all_to_all x1, starting transfers between devices, per_device(): lax.all_to_all(outgoing, ('dp', 'mp'), split_axis=1, concat_axis=1, tiled...  11.5 us
    all_to_all x1, starting transfers between devices, per_device(): lax.all_to_all(leaving, ('dp', 'mp'), split_axis=1, concat_axis=1, tiled=...  6.38 us
    reshape x2, local copies, waits for them, and re-layouts, per_device(): leaving = result.reshape(capacity, devices, row_share, block_size)  5.29 us
  transfers between devices with their start and end apart: 2, of which 1 were waited for; matrix products, arithmetic and copies ran while one was open for 1% of the time, Pallas kernels for 0%

commit v1 on v0

v1 whole, which is shorter than its diff:
```python
import math

import jax
import jax.numpy as jnp
from jax import lax
from jax.experimental import pallas as pl
from jax.experimental.pallas import tpu as pltpu
from jax.sharding import PartitionSpec as P

STAT_DECAY = 0.95
CLIP_SHARE = 0.5
EPSILON = 1e-06

B = 512
NBLK = 128
CAP = 2
NDEV = 128
DP = 8
MP = 16
ROWS = B // NDEV
WIDE = B + 128
LEVELS = 32766.0
STEPS = 64.0

BF16 = jnp.bfloat16
F32 = jnp.float32
MESH = pl.DeviceIdType.MESH

C5 = [1.25 ** (5 - k) * (-0.25) ** k * math.comb(5, k) for k in range(6)]
V = [1.5625, -0.3125, 0.0, 0.0, 0.0, 0.0, 0.0]
for _k in range(6):
    V[_k + 1] -= C5[_k] / 4


def dot(former, latter):
    return jnp.dot(former, latter, preferred_element_type=F32)


def split(value):
    high = value.astype(BF16)
    return high, (value - high.astype(F32)).astype(BF16)


def total(value):
    return jnp.sum(jnp.sum(value, axis=0, keepdims=True), axis=1, keepdims=True)


def partner(step):
    dp, mp = lax.axis_index("dp"), lax.axis_index("mp")
    offset = lax.rem(step * 59, NDEV)
    core = lax.rem(lax.rem(dp, 2) + lax.rem(offset, 2), 2)
    z = lax.rem(lax.div(dp, 2) + lax.rem(lax.div(offset, 2), 4), 4)
    y = lax.rem(lax.div(mp, 4) + lax.rem(lax.div(offset, 8), 4), 4)
    x = lax.rem(lax.rem(mp, 4) + lax.div(offset, 32), 4)
    return z * 2 + core, y * 4 + x


def roots_and_product(g, sl, sr, nl, nr, squared, live, three, s):
    fs = []
    for side, (stat, fresh) in enumerate(((sl, nl), (sr, nr))):
        dims = (((1,), (1,)), ((), ())) if side == 0 else (((0,), (0,)), ((), ()))
        gram = lax.dot_general(g[...], g[...], dims, preferred_element_type=F32)
        old = stat[...]
        a = STAT_DECAY * old + squared * gram
        a = jnp.where(live, a, old)
        fresh[...] = a
        fs.append(1.0 / jnp.sqrt(total(a * a)))
    a_of = (nl, nr)
    both = (0, 1)
    for i in both:
        s["mh"][i], s["ml"][i] = split(a_of[i][...] * fs[i])
    for i in both:
        square = dot(s["mh"][i], s["mh"][i])
        s["d"][i] = (a_of[i][...] * (-0.625 * fs[i]) + square * 0.0625).astype(BF16)
    for i in both:
        f = s["d"][i].astype(F32) * 3.125 + dot(s["d"][i], s["d"][i])
        s["fh"][i], s["fl"][i] = split(f)
    for i in both:
        n = (
            a_of[i][...] * (1.25**4 * fs[i])
            + dot(s["fh"][i], s["mh"][i])
            + dot(s["fh"][i], s["ml"][i])
            + dot(s["fl"][i], s["mh"][i])
        )
        s["n"][i] = n
        s["nh"][i], s["nl"][i] = split(n)
    for i in both:
        square = dot(s["nh"][i], s["nh"][i]) + dot(s["nh"][i], s["nl"][i]) + dot(s["nl"][i], s["nh"][i])
        s["s"][i] = square.astype(BF16)
    for i in both:
        c = dot(s["s"][i], s["nh"][i])
        s["c"][i] = c.astype(BF16)
        s["b"][i] = (V[4] * s["nh"][i].astype(F32) + V[5] * s["s"][i].astype(F32) + V[6] * c).astype(BF16)
    w0, w1 = jnp.where(three, V[0], 1.25), jnp.where(three, V[1], -0.25)
    w2, w3, w4 = jnp.where(three, V[2], 0.0), jnp.where(three, V[3], 0.0), jnp.where(three, 1.0, 0.0)
    for i in both:
        u = (
            w1 * s["n"][i]
            + w2 * s["s"][i].astype(F32)
            + w3 * s["c"][i].astype(F32)
            + w4 * dot(s["c"][i], s["b"][i])
        )
        s["n"][i] = u
        s["u"][i] = u.astype(BF16)
    for i in both:
        z = 1.25 * s["n"][i] - a_of[i][...] * (fs[i] * w0 * 0.25) - 0.25 * dot(s["mh"][i], s["u"][i])
        s["zh"][i], s["zl"][i] = split(z)
    alpha = 1.25 * w0
    h = alpha * g[...].astype(F32) + dot(s["zh"][0], g[...]) + dot(s["zl"][0], g[...])
    s["p"][...] = h
    s["hh"][...], s["hl"][...] = split(h)
    p = (
        alpha * s["p"][...]
        + dot(s["hh"][...], s["zh"][1])
        + dot(s["hh"][...], s["zl"][1])
        + dot(s["hl"][...], s["zh"][1])
    )
    s["p"][...] = p
    return total(p * p)


PAIRS = [
    ("mh", BF16), ("ml", BF16), ("d", BF16), ("fh", BF16), ("fl", BF16), ("n", F32), ("nh", BF16), ("nl", BF16),
    ("s", BF16), ("c", BF16), ("b", BF16), ("u", BF16), ("zh", BF16), ("zl", BF16),
]
SINGLES = [("hh", BF16), ("hl", BF16), ("p", F32), ("g", BF16)]
NAMES = [name for name, _ in PAIRS + SINGLES]


def kernel(
    plan, where, grads, left_hbm, right_hbm, update, new_left_hbm, new_right_hbm,
    left, right, new_left, new_right, fsend, frecv, rsend, rrecv,
    local_sem, out_sem, fs_sem, fr_sem, rs_sem, rr_sem, round_sem, *rest,
):
    s = dict(zip(NAMES, rest, strict=True))
    dp, mp = lax.axis_index("dp"), lax.axis_index("mp")
    me = dp * MP + mp

    barrier = pltpu.get_barrier_semaphore()
    for k in range(1, DP):
        pl.semaphore_signal(barrier, inc=1, device_id=(lax.rem(dp + k, DP), mp), device_id_type=MESH)
    for k in range(1, MP):
        pl.semaphore_signal(barrier, inc=1, device_id=(dp, lax.rem(mp + k, MP)), device_id_type=MESH)

    loads = [
        pltpu.make_async_copy(left_hbm, left, local_sem.at[0]),
        pltpu.make_async_copy(right_hbm, right, local_sem.at[1]),
    ]
    for load in loads:
        load.start()

    def place(owner, carry):
        for j in range(CAP):
            fsend[j, owner, :, 0:B] = grads[lax.div(plan[owner * CAP + j], 4)]
        return carry

    lax.fori_loop(0, NDEV, place, 0, unroll=8)

    widened = grads[...].astype(F32)
    mine = jnp.broadcast_to(total(jnp.sum(widened * widened, axis=0)), (ROWS, 128))
    part0 = mine.astype(BF16).astype(F32)
    part1 = (mine - part0).astype(BF16).astype(F32)
    part2 = mine - part0 - part1
    row = lax.broadcasted_iota(jnp.int32, (ROWS, 128), 0)
    parts = jnp.where(row == 0, part0, jnp.where(row == 1, part1, jnp.where(row == 2, part2, 0.0)))
    tail = jnp.broadcast_to(parts.astype(BF16)[None], (NDEV, ROWS, 128))
    for j in range(CAP):
        fsend[j, :, :, B:WIDE] = tail
        frecv[j, me] = fsend[j, me]

    pl.semaphore_wait(barrier, DP + MP - 2)
    for k in range(1, MP):
        pl.semaphore_signal(round_sem, inc=1, device_id=(dp, lax.rem(mp + k, MP)), device_id_type=MESH)
    pl.semaphore_wait(round_sem, MP - 1)

    def exchange(source, target, j, send_sem, recv_sem):
        def step(k, carry):
            to_dp, to_mp = partner(k)
            pltpu.make_async_remote_copy(
                src_ref=source.at[j, to_dp * MP + to_mp],
                dst_ref=target.at[j, me],
                send_sem=send_sem.at[j],
                recv_sem=recv_sem.at[j],
                device_id=(to_dp, to_mp),
                device_id_type=MESH,
            ).start()
            return carry

        lax.fori_loop(1, NDEV, step, 0)

    def settle(buffer, j, sem):
        view = buffer.at[j, pl.ds(0, NDEV - 1)]
        pltpu.make_async_copy(view, view, sem.at[j]).wait()

    for j in range(CAP):
        exchange(fsend, frecv, j, fs_sem, fr_sem)
    for load in loads:
        load.wait()

    def slot(j, carry):
        settle(frecv, j, fr_sem)
        arrived = frecv[j, :, :, 0:B].reshape(B, B)
        s["g"][...] = arrived
        wide = arrived.astype(F32)
        grad_square = total(wide * wide)
        square_sum = total(jnp.sum(frecv[j, :, :, B : B + 128].astype(F32), axis=0)) * (1.0 / 128)
        clipping = jnp.minimum(
            1.0, CLIP_SHARE * B * math.sqrt(NBLK) / (jnp.sqrt(square_sum) + EPSILON)
        )
        granted = lax.rem(plan[me * CAP + j], 4)
        prod_square = roots_and_product(
            s["g"], left.at[j], right.at[j], new_left.at[j], new_right.at[j],
            clipping * clipping, granted > 0, granted > 2, s,
        )
        pltpu.make_async_copy(new_left.at[j], new_left_hbm.at[j], out_sem.at[0, j]).start()
        pltpu.make_async_copy(new_right.at[j], new_right_hbm.at[j], out_sem.at[1, j]).start()
        graft = clipping * jnp.sqrt(grad_square) / (jnp.sqrt(prod_square) + EPSILON)
        scaled = s["p"][...] * graft
        largest = jnp.maximum(jnp.max(jnp.abs(scaled), axis=1, keepdims=True), 1e-30)
        code = jnp.ceil(jnp.log2(largest * (1.0 / LEVELS)) * STEPS)
        levels = jnp.round(scaled * jnp.exp2(code * (-1.0 / STEPS)))
        rsend[j, :, :, 0:B] = levels.astype(jnp.int32).astype(jnp.int16).reshape(NDEV, ROWS, B)
        codes = jnp.broadcast_to(code.astype(jnp.int32), (B, 128)).astype(jnp.int16)
        rsend[j, :, :, B:WIDE] = codes.reshape(NDEV, ROWS, 128)
        rrecv[j, me] = rsend[j, me]
        exchange(rsend, rrecv, j, rs_sem, rr_sem)
        return carry

    lax.fori_loop(0, CAP, slot, 0)

    for j in range(CAP):
        settle(rrecv, j, rr_sem)

    def gather(b, carry):
        at = where[b]
        piece = rrecv[lax.rem(at, CAP), lax.div(at, CAP)]
        scale = jnp.exp2(piece[:, B:WIDE].astype(jnp.int32).astype(F32) * (1.0 / STEPS))
        values = piece[:, 0:B].astype(jnp.int32).astype(F32)
        update[b] = values * jnp.concatenate([scale] * (B // 128), axis=1)
        return carry

    lax.fori_loop(0, NBLK, gather, 0, unroll=8)

    for j in range(CAP):
        pltpu.make_async_copy(new_left.at[j], new_left_hbm.at[j], out_sem.at[0, j]).wait()
        pltpu.make_async_copy(new_right.at[j], new_right_hbm.at[j], out_sem.at[1, j]).wait()
        settle(fsend, j, fs_sem)
        settle(rsend, j, rs_sem)


def per_device(grads, block_slot, iters_count, stat_left, stat_right):
    slots = jnp.arange(CAP * NDEV, dtype=jnp.int32)
    marks = jnp.arange(NBLK, dtype=jnp.int32) * 4 + iters_count
    plan = jnp.sum(jnp.where(slots[:, None] == block_slot[None, :], marks[None, :], 0), axis=1)
    smem, vmem, hbm = (pl.BlockSpec(memory_space=m) for m in (pltpu.SMEM, pltpu.VMEM, pl.ANY))
    dma = pltpu.SemaphoreType.DMA
    return pl.pallas_call(
        kernel,
        out_shape=(
            jax.ShapeDtypeStruct((NBLK, ROWS, B), F32),
            jax.ShapeDtypeStruct((CAP, B, B), F32),
            jax.ShapeDtypeStruct((CAP, B, B), F32),
        ),
        in_specs=[smem, smem, vmem, hbm, hbm],
        out_specs=(vmem, hbm, hbm),
        scratch_shapes=[pltpu.VMEM((CAP, B, B), F32)] * 4
        + [pltpu.VMEM((CAP, NDEV, ROWS, WIDE), BF16)] * 2
        + [pltpu.VMEM((CAP, NDEV, ROWS, WIDE), jnp.int16)] * 2
        + [dma((2,)), dma((2, CAP))]
        + [dma((CAP,))] * 4
        + [pltpu.SemaphoreType.REGULAR]
        + [pltpu.VMEM((2, B, B), t) for _, t in PAIRS]
        + [pltpu.VMEM((B, B), t) for _, t in SINGLES],
        compiler_params=pltpu.CompilerParams(
            collective_id=0, has_side_effects=True, vmem_limit_bytes=56 * 2**20
        ),
    )(plan, block_slot, grads, stat_left, stat_right)


def solution(mesh):
    in_specs = (
        P(None, ("dp", "mp"), None),
        P(),
        P(),
        P(("dp", "mp"), None, None),
        P(("dp", "mp"), None, None),
    )
    out_specs = (
        P(None, ("dp", "mp"), None),
        P(("dp", "mp"), None, None),
        P(("dp", "mp"), None, None),
    )
    return jax.shard_map(
        per_device, mesh=mesh, in_specs=in_specs, out_specs=out_specs, check_vma=False
    )
```

time: 226 us -> 69.1 us (0.31); the launches traced: 221 us -> 68.9 us
  matrix products: 81.3 us -> 0 us
  blocking collectives: 69.3 us -> 0 us
  Pallas kernels: 0 us -> 60.1 us
  waiting for transfers between devices: 29.6 us -> 0 us
  starting transfers between devices: 17.9 us -> 0 us
  local copies, waits for them, and re-layouts: 15.1 us -> 6.08 us
  other arithmetic: 6.29 us -> 1.99 us
    dot_general x14 -> x0, matrix products: 81.3 us -> none  [the longest x11 75.4 us: batched(): return jnp.matmul(former, latter, precision=lax.Precision.HIGHEST)]
    psum x1 -> x0, blocking collectives: 69.3 us -> none  [per_device(): square_sum = lax.psum(jnp.sum(widened_rows * widened_rows), ('dp', 'mp'))]
    pallas_call x0 -> x1, Pallas kernels: none -> 60.1 us  [per_device(): pl.pallas_call(kernel, out_shape=(jax.ShapeDtypeStruct((NBLK, ROWS, B), F...]
    all_to_all x2 -> x0, waiting for transfers between devices: 29.6 us -> none  [the longest x1 29.6 us: per_device(): lax.all_to_all(leaving, ('dp', 'mp'), split_axis=1, concat_axis=1, tiled=...]
    all_to_all x2 -> x0, starting transfers between devices: 17.9 us -> none  [the longest x1 11.5 us: per_device(): lax.all_to_all(outgoing, ('dp', 'mp'), split_axis=1, concat_axis=1, tiled...]
    reshape x5 -> x0, local copies, waits for them, and re-layouts: 9.28 us -> none  [the longest x2 5.29 us: per_device(): leaving = result.reshape(capacity, devices, row_share, block_size)]
    unnamed x16 -> x7, local copies, waits for them, and re-layouts: 2.38 us -> 6.08 us
  transfers between devices with their start and end apart: 2 -> 0, of which waited for: 1 -> 0; matrix products, arithmetic and copies ran while one was open for 1% -> 0% of each run, Pallas kernels for 0% -> 0%
where the time goes in v1:
time: 69.1 us; the launch traced here: 68.9 us
  Pallas kernels  60.1 us (87%)
  local copies, waits for them, and re-layouts  6.08 us (9%)
  other arithmetic  1.99 us (3%)
    pallas_call x1, Pallas kernels, per_device(): pl.pallas_call(kernel, out_shape=(jax.ShapeDtypeStruct((NBLK, ROWS, B), F...  60.1 us
    unnamed x7, local copies, waits for them, and re-layouts  6.08 us

profile of v1, /device:TPU:1, one launch (start us, length us, event | category | flops | bytes accessed | tf_op | source)
XLA Modules:
  0.0 68.9 jit_solution(13889877692186692048)
XLA Ops:
  0.6 0.7 multiply_add_fusion
  1.3 1.3 %select_reduce_fusion.plan = s32[256]{0:T(256)} fusion(s32[128]{0:T(128)S(1)} %multiply_add_fusion, s32[128]{0:T(128)} %where.1), kind=kLoop, calls=%fused_computation | loop fusion | flops 98048 | bytes 2048 | tf_op jit(solution)/shard_map/reduce_sum | solution.py:254
  2.6 60.1 %shard_map.76 = (f32[128,4,512]{2,1,0:T(4,128)}, f32[2,512,512]{2,1,0:T(8,128)}, f32[2,512,512]{2,1,0:T(8,128)}) custom-call(s32[256]{0:T(256)} %select_reduce_fusion.plan, s32[128]{0:T(128)} %where.1, bf16[128,4,512]{2,1,0:T(4,128)(2,1)} %grads.1, f32[2,512,512]{2,1,0:T(8,128)} %left_hbm.1, f32[2,512,512]{2,1,0:T(8,128)} %right_hbm.1), custom_call_target="tpu_custom_call" | custom-call | tf_op jit(solution)/shard_map/pallas_call | solution.py:257
  62.8 0.0 copy-start.1
  62.8 2.4 %copy.11 = f32[128,4,512]{2,1,0:T(4,128)} copy(f32[128,4,512]{2,1,0:T(4,128)} %get-tuple-element.6) | data formatting | bytes 2097152
  65.2 0.0 copy-done.1
  65.2 0.0 copy-start
  65.2 1.3 %copy.12 = f32[2,512,512]{2,1,0:T(8,128)} copy(f32[2,512,512]{2,1,0:T(8,128)S(1)} %copy-done.1) | data formatting | bytes 4194304
  66.5 1.0 %copy-done = f32[2,512,512]{2,1,0:T(8,128)S(1)} copy-done((f32[2,512,512]{2,1,0:T(8,128)S(1)}, f32[2,512,512]{2,1,0:T(8,128)}, u32[]{:S(2)}) %copy-start) | copy-done | bytes 2097176
  67.6 1.3 %copy.13 = f32[2,512,512]{2,1,0:T(8,128)} copy(f32[2,512,512]{2,1,0:T(8,128)S(1)} %copy-done) | data formatting | bytes 4194304
Async XLA Ops:
  62.8 2.4 %copy-start.1 = (f32[2,512,512]{2,1,0:T(8,128)S(1)}, f32[2,512,512]{2,1,0:T(8,128)}, u32[]{:S(2)}) copy-start(f32[2,512,512]{2,1,0:T(8,128)} %get-tuple-element.7) | copy-start | bytes 6291460
  65.2 2.3 %copy-start = (f32[2,512,512]{2,1,0:T(8,128)S(1)}, f32[2,512,512]{2,1,0:T(8,128)}, u32[]{:S(2)}) copy-start(f32[2,512,512]{2,1,0:T(8,128)} %get-tuple-element.8) | copy-start | bytes 6291460

commit v2 on v1

--- a/solution.py
+++ b/solution.py
@@ -21,6 +21,7 @@
 WIDE = B + 128
 LEVELS = 32766.0
 STEPS = 64.0
+UNROLL = 127
 
 BF16 = jnp.bfloat16
 F32 = jnp.float32
@@ -47,11 +48,11 @@
 
 def partner(step):
     dp, mp = lax.axis_index("dp"), lax.axis_index("mp")
-    offset = lax.rem(step * 59, NDEV)
-    core = lax.rem(lax.rem(dp, 2) + lax.rem(offset, 2), 2)
-    z = lax.rem(lax.div(dp, 2) + lax.rem(lax.div(offset, 2), 4), 4)
-    y = lax.rem(lax.div(mp, 4) + lax.rem(lax.div(offset, 8), 4), 4)
-    x = lax.rem(lax.rem(mp, 4) + lax.div(offset, 32), 4)
+    offset = (step * 59) & (NDEV - 1)
+    core = (dp + offset) & 1
+    z = ((dp >> 1) + (offset >> 1)) & 3
+    y = ((mp >> 2) + (offset >> 3)) & 3
+    x = (mp + (offset >> 5)) & 3
     return z * 2 + core, y * 4 + x
 
 
@@ -128,9 +129,9 @@
 
 
 def kernel(
-    plan, where, grads, left_hbm, right_hbm, update, new_left_hbm, new_right_hbm,
-    left, right, new_left, new_right, fsend, frecv, rsend, rrecv,
-    local_sem, out_sem, fs_sem, fr_sem, rs_sem, rr_sem, round_sem, *rest,
+    slot_hbm, counts_hbm, grads_hbm, left_hbm, right_hbm, returned, new_left_hbm, new_right_hbm,
+    slot_of, counts, grads, left, right, new_left, new_right, fsend, frecv, rsend, psend, precv, gsend, grecv, plan_v, plan,
+    local_sem, out_sem, fs_sem, fr_sem, rs_sem, rr_sem, ps_sem, pr_sem, round_sem, *rest,
 ):
     s = dict(zip(NAMES, rest, strict=True))
     dp, mp = lax.axis_index("dp"), lax.axis_index("mp")
@@ -138,39 +139,59 @@
 
     barrier = pltpu.get_barrier_semaphore()
     for k in range(1, DP):
-        pl.semaphore_signal(barrier, inc=1, device_id=(lax.rem(dp + k, DP), mp), device_id_type=MESH)
+        pl.semaphore_signal(barrier, inc=1, device_id=((dp + k) & (DP - 1), mp), device_id_type=MESH)
     for k in range(1, MP):
-        pl.semaphore_signal(barrier, inc=1, device_id=(dp, lax.rem(mp + k, MP)), device_id_type=MESH)
-
+        pl.semaphore_signal(barrier, inc=1, device_id=(dp, (mp + k) & (MP - 1)), device_id_type=MESH)
+
+    tables = [
+        pltpu.make_async_copy(slot_hbm, slot_of, local_sem.at[2]),
+        pltpu.make_async_copy(counts_hbm, counts, local_sem.at[3]),
+    ]
+    rows = pltpu.make_async_copy(grads_hbm, grads, local_sem.at[4])
     loads = [
         pltpu.make_async_copy(left_hbm, left, local_sem.at[0]),
         pltpu.make_async_copy(right_hbm, right, local_sem.at[1]),
     ]
-    for load in loads:
+    for load in [*tables, rows, *loads]:
         load.start()
+    for load in tables:
+        load.wait()
+
+    lane = lax.broadcasted_iota(jnp.int32, (NBLK, NBLK), 1)
+    marks = jnp.transpose(lane * 4 + jnp.broadcast_to(counts[...] & 3, (NBLK, NBLK)))
+    named = jnp.transpose(jnp.broadcast_to(slot_of[...], (NBLK, NBLK)))
+    for half in range(CAP):
+        found = jnp.where(named == lane + half * NBLK, marks, 0)
+        plan_v[pl.ds(half, 1), :] = jnp.max(found, axis=0, keepdims=True)
+    to_scalars = pltpu.make_async_copy(plan_v, plan, local_sem.at[5])
+    to_scalars.start()
+
+    rows.wait()
+    widened = grads[...].astype(F32)
+    mine = jnp.sum(widened * widened, axis=0)
+    psend[...] = mine[:, 0:128] + mine[:, 128:256] + mine[:, 256:384] + mine[:, 384:512]
+    precv[dp] = psend[...]
+
+    to_scalars.wait()
 
     def place(owner, carry):
         for j in range(CAP):
-            fsend[j, owner, :, 0:B] = grads[lax.div(plan[owner * CAP + j], 4)]
+            at = owner * CAP + j
+            fsend[j, owner] = grads[jnp.minimum(plan[at >> 7, at & (NBLK - 1)] >> 2, NBLK - 1)]
         return carry
 
     lax.fori_loop(0, NDEV, place, 0, unroll=8)
-
-    widened = grads[...].astype(F32)
-    mine = jnp.broadcast_to(total(jnp.sum(widened * widened, axis=0)), (ROWS, 128))
-    part0 = mine.astype(BF16).astype(F32)
-    part1 = (mine - part0).astype(BF16).astype(F32)
-    part2 = mine - part0 - part1
-    row = lax.broadcasted_iota(jnp.int32, (ROWS, 128), 0)
-    parts = jnp.where(row == 0, part0, jnp.where(row == 1, part1, jnp.where(row == 2, part2, 0.0)))
-    tail = jnp.broadcast_to(parts.astype(BF16)[None], (NDEV, ROWS, 128))
     for j in range(CAP):
-        fsend[j, :, :, B:WIDE] = tail
         frecv[j, me] = fsend[j, me]
 
     pl.semaphore_wait(barrier, DP + MP - 2)
     for k in range(1, MP):
-        pl.semaphore_signal(round_sem, inc=1, device_id=(dp, lax.rem(mp + k, MP)), device_id_type=MESH)
+        pl.semaphore_signal(round_sem, inc=1, device_id=(dp, (mp + k) & (MP - 1)), device_id_type=MESH)
+    for k in range(1, DP):
+        pltpu.make_async_remote_copy(
+            src_ref=psend, dst_ref=precv.at[dp], send_sem=ps_sem.at[0], recv_sem=pr_sem.at[0],
+            device_id=((dp + k) & (DP - 1), mp), device_id_type=MESH,
+        ).start()
     pl.semaphore_wait(round_sem, MP - 1)
 
     def exchange(source, target, j, send_sem, recv_sem):
@@ -186,28 +207,40 @@
             ).start()
             return carry
 
-        lax.fori_loop(1, NDEV, step, 0)
-
-    def settle(buffer, j, sem):
-        view = buffer.at[j, pl.ds(0, NDEV - 1)]
-        pltpu.make_async_copy(view, view, sem.at[j]).wait()
-
-    for j in range(CAP):
-        exchange(fsend, frecv, j, fs_sem, fr_sem)
+        lax.fori_loop(1, NDEV, step, 0, unroll=UNROLL)
+
+    def settle(view, sem):
+        pltpu.make_async_copy(view, view, sem).wait()
+
+    def others(buffer, j):
+        return buffer.at[j, pl.ds(0, NDEV - 1)]
+
+    exchange(fsend, frecv, 0, fs_sem, fr_sem)
+    settle(precv.at[pl.ds(0, DP - 1)], pr_sem.at[0])
+    gsend[...] = jnp.sum(precv[...], axis=0)
+    grecv[mp] = gsend[...]
+    for k in range(1, MP):
+        pltpu.make_async_remote_copy(
+            src_ref=gsend, dst_ref=grecv.at[mp], send_sem=ps_sem.at[1], recv_sem=pr_sem.at[1],
+            device_id=(dp, (mp + k) & (MP - 1)), device_id_type=MESH,
+        ).start()
+    exchange(fsend, frecv, 1, fs_sem, fr_sem)
     for load in loads:
         load.wait()
+    settle(grecv.at[pl.ds(0, MP - 1)], pr_sem.at[1])
 
     def slot(j, carry):
-        settle(frecv, j, fr_sem)
-        arrived = frecv[j, :, :, 0:B].reshape(B, B)
+        settle(others(frecv, j), fr_sem.at[j])
+        arrived = frecv[j].reshape(B, B)
         s["g"][...] = arrived
         wide = arrived.astype(F32)
         grad_square = total(wide * wide)
-        square_sum = total(jnp.sum(frecv[j, :, :, B : B + 128].astype(F32), axis=0)) * (1.0 / 128)
+        square_sum = total(jnp.sum(grecv[...], axis=0))
         clipping = jnp.minimum(
             1.0, CLIP_SHARE * B * math.sqrt(NBLK) / (jnp.sqrt(square_sum) + EPSILON)
         )
-        granted = lax.rem(plan[me * CAP + j], 4)
+        my_slot = me * CAP + j
+        granted = plan[my_slot >> 7, my_slot & (NBLK - 1)] & 3
         prod_square = roots_and_product(
             s["g"], left.at[j], right.at[j], new_left.at[j], new_right.at[j],
             clipping * clipping, granted > 0, granted > 2, s,
@@ -222,59 +255,79 @@
         rsend[j, :, :, 0:B] = levels.astype(jnp.int32).astype(jnp.int16).reshape(NDEV, ROWS, B)
         codes = jnp.broadcast_to(code.astype(jnp.int32), (B, 128)).astype(jnp.int16)
         rsend[j, :, :, B:WIDE] = codes.reshape(NDEV, ROWS, 128)
-        rrecv[j, me] = rsend[j, me]
-        exchange(rsend, rrecv, j, rs_sem, rr_sem)
+        exchange(rsend, returned, j, rs_sem, rr_sem)
+        pltpu.make_async_copy(rsend.at[j, me], returned.at[j, me], out_sem.at[2, j]).start()
         return carry
 
     lax.fori_loop(0, CAP, slot, 0)
 
     for j in range(CAP):
-        settle(rrecv, j, rr_sem)
+        pltpu.make_async_copy(new_left.at[j], new_left_hbm.at[j], out_sem.at[0, j]).wait()
+        pltpu.make_async_copy(new_right.at[j], new_right_hbm.at[j], out_sem.at[1, j]).wait()
+        pltpu.make_async_copy(rsend.at[j, me], returned.at[j, me], out_sem.at[2, j]).wait()
+        settle(others(fsend, j), fs_sem.at[j])
+        settle(others(rsend, j), rs_sem.at[j])
+    settle(precv.at[pl.ds(0, DP - 1)], ps_sem.at[0])
+    settle(grecv.at[pl.ds(0, MP - 1)], ps_sem.at[1])
+    for j in range(CAP):
+        settle(others(returned, j), rr_sem.at[j])
+
+
+def finish(slot_of, returned, left, right, update, new_left, new_right, sems):
+    copies = [
+        pltpu.make_async_copy(left, new_left, sems.at[0]),
+        pltpu.make_async_copy(right, new_right, sems.at[1]),
+    ]
+    for copy in copies:
+        copy.start()
 
     def gather(b, carry):
-        at = where[b]
-        piece = rrecv[lax.rem(at, CAP), lax.div(at, CAP)]
+        at = slot_of[b]
+        piece = returned[at & 1, at >> 1]
         scale = jnp.exp2(piece[:, B:WIDE].astype(jnp.int32).astype(F32) * (1.0 / STEPS))
         values = piece[:, 0:B].astype(jnp.int32).astype(F32)
         update[b] = values * jnp.concatenate([scale] * (B // 128), axis=1)
         return carry
 
     lax.fori_loop(0, NBLK, gather, 0, unroll=8)
-
-    for j in range(CAP):
-        pltpu.make_async_copy(new_left.at[j], new_left_hbm.at[j], out_sem.at[0, j]).wait()
-        pltpu.make_async_copy(new_right.at[j], new_right_hbm.at[j], out_sem.at[1, j]).wait()
-        settle(fsend, j, fs_sem)
-        settle(rsend, j, rs_sem)
+    for copy in copies:
+        copy.wait()
 
 
 def per_device(grads, block_slot, iters_count, stat_left, stat_right):
-    slots = jnp.arange(CAP * NDEV, dtype=jnp.int32)
-    marks = jnp.arange(NBLK, dtype=jnp.int32) * 4 + iters_count
-    plan = jnp.sum(jnp.where(slots[:, None] == block_slot[None, :], marks[None, :], 0), axis=1)
     smem, vmem, hbm = (pl.BlockSpec(memory_space=m) for m in (pltpu.SMEM, pltpu.VMEM, pl.ANY))
     dma = pltpu.SemaphoreType.DMA
-    return pl.pallas_call(
+    stats = jax.ShapeDtypeStruct((CAP, B, B), F32)
+    returned, left, right = pl.pallas_call(
         kernel,
-        out_shape=(
-            jax.ShapeDtypeStruct((NBLK, ROWS, B), F32),
-            jax.ShapeDtypeStruct((CAP, B, B), F32),
-            jax.ShapeDtypeStruct((CAP, B, B), F32),
-        ),
-        in_specs=[smem, smem, vmem, hbm, hbm],
-        out_specs=(vmem, hbm, hbm),
-        scratch_shapes=[pltpu.VMEM((CAP, B, B), F32)] * 4
-        + [pltpu.VMEM((CAP, NDEV, ROWS, WIDE), BF16)] * 2
-        + [pltpu.VMEM((CAP, NDEV, ROWS, WIDE), jnp.int16)] * 2
-        + [dma((2,)), dma((2, CAP))]
-        + [dma((CAP,))] * 4
+        out_shape=(jax.ShapeDtypeStruct((CAP, NDEV, ROWS, WIDE), jnp.int16), stats, stats),
+        in_specs=[hbm] * 5,
+        out_specs=(hbm, hbm, hbm),
+        scratch_shapes=[pltpu.VMEM((1, NBLK), jnp.int32)] * 2
+        + [pltpu.VMEM((NBLK, ROWS, B), BF16)]
+        + [pltpu.VMEM((CAP, B, B), F32)] * 4
+        + [pltpu.VMEM((CAP, NDEV, ROWS, B), BF16)] * 2
+        + [pltpu.VMEM((CAP, NDEV, ROWS, WIDE), jnp.int16)]
+        + [pltpu.VMEM((ROWS, 128), F32), pltpu.VMEM((DP, ROWS, 128), F32)]
+        + [pltpu.VMEM((ROWS, 128), F32), pltpu.VMEM((MP, ROWS, 128), F32)]
+        + [pltpu.VMEM((CAP, NBLK), jnp.int32), pltpu.SMEM((CAP, NBLK), jnp.int32)]
+        + [dma((6,)), dma((3, CAP))]
+        + [dma((CAP,))] * 6
         + [pltpu.SemaphoreType.REGULAR]
         + [pltpu.VMEM((2, B, B), t) for _, t in PAIRS]
         + [pltpu.VMEM((B, B), t) for _, t in SINGLES],
         compiler_params=pltpu.CompilerParams(
             collective_id=0, has_side_effects=True, vmem_limit_bytes=56 * 2**20
         ),
-    )(plan, block_slot, grads, stat_left, stat_right)
+    )(block_slot.reshape(1, NBLK), iters_count.reshape(1, NBLK), grads, stat_left, stat_right)
+    return pl.pallas_call(
+        finish,
+        out_shape=(jax.ShapeDtypeStruct((NBLK, ROWS, B), F32), stats, stats),
+        in_specs=[smem, vmem, hbm, hbm],
+        out_specs=(vmem, hbm, hbm),
+        scratch_shapes=[dma((2,))],
+        compiler_params=pltpu.CompilerParams(vmem_limit_bytes=16 * 2**20),
+    )(block_slot, returned, left, right)
 
 
 def solution(mesh):

time: 69.1 us -> 63.2 us (0.915)
  Pallas kernels: 60.1 us -> 57.8 us
  other arithmetic: 1.99 us -> 0 us
  local copies, waits for them, and re-layouts: 6.08 us -> 4.49 us
    pallas_call x1 -> x2, Pallas kernels: 60.1 us -> 57.8 us  [the longest x1 54.3 us: per_device(): pl.pallas_call(kernel, out_shape=(jax.ShapeDtypeStruct((CAP, NDEV, ROWS,...]
    unnamed x7 -> x8, local copies, waits for them, and re-layouts: 6.08 us -> 4.49 us
    reduce_sum x1 -> x0, other arithmetic: 1.33 us -> none  [per_device(): jnp.sum(jnp.where(slots[:, None] == block_slot[None, :], marks[None, :],...]
where the time goes in v2:
time: 63.2 us; the launch traced here: 63 us
  Pallas kernels  57.8 us (91%)
  local copies, waits for them, and re-layouts  4.49 us (7%)
  between operations  0.67 us (1%)
    pallas_call x1, Pallas kernels, per_device(): pl.pallas_call(kernel, out_shape=(jax.ShapeDtypeStruct((CAP, NDEV, ROWS,...  54.3 us
    unnamed x8, local copies, waits for them, and re-layouts  4.49 us
    pallas_call x1, Pallas kernels, per_device(): pl.pallas_call(finish, out_shape=(jax.ShapeDtypeStruct((NBLK, ROWS, B), F...  3.53 us

profile of v2, /device:TPU:1, one launch (start us, length us, event | category | flops | bytes accessed | tf_op | source)
XLA Modules:
  0.0 63.0 jit_solution(2330914293093286912)
XLA Ops:
  0.6 0.0 copy-start.3
  0.6 54.3 %shard_map.76 = (s16[2,128,4,640]{3,2,1,0:T(4,128)(2,1)}, f32[2,512,512]{2,1,0:T(8,128)}, f32[2,512,512]{2,1,0:T(8,128)}) custom-call(s32[1,128]{1,0:T(1,128)} %bitcast.2, s32[1,128]{1,0:T(1,128)} %bitcast.3, bf16[128,4,512]{2,1,0:T(4,128)(2,1)} %grads_hbm.1, f32[2,512,512]{2,1,0:T(8,128)} %left_hbm.1, f32[2,512,512]{2,1,0:T(8,128)} %right_hbm.1), custom_call_target="tpu_custom_call" | custom-call | tf_op jit(solution)/shard_map/pallas_call | solution.py:301
  54.9 0.0 copy-done.3
  55.0 0.0 copy-start
  55.0 1.6 %copy-done = f32[2,512,512]{2,1,0:T(8,128)S(1)} copy-done((f32[2,512,512]{2,1,0:T(8,128)S(1)}, f32[2,512,512]{2,1,0:T(8,128)}, u32[]{:S(2)}) %copy-start) | copy-done | bytes 2097176
  56.5 0.0 copy-start.1
  56.5 1.6 %copy-done.1 = f32[2,512,512]{2,1,0:T(8,128)S(1)} copy-done((f32[2,512,512]{2,1,0:T(8,128)S(1)}, f32[2,512,512]{2,1,0:T(8,128)}, u32[]{:S(2)}) %copy-start.1) | copy-done | bytes 2097176
  58.1 0.0 copy-start.2
  58.1 1.3 %copy-done.2 = s16[2,128,4,640]{3,2,1,0:T(4,128)(2,1)S(1)} copy-done((s16[2,128,4,640]{3,2,1,0:T(4,128)(2,1)S(1)}, s16[2,128,4,640]{3,2,1,0:T(4,128)(2,1)}, u32[]{:S(2)}) %copy-start.2) | copy-done | bytes 1310744
  59.5 3.5 %shard_map.77 = (f32[128,4,512]{2,1,0:T(4,128)}, f32[2,512,512]{2,1,0:T(8,128)}, f32[2,512,512]{2,1,0:T(8,128)}) custom-call(s32[128]{0:T(128)S(1)} %copy-done.3, s16[2,128,4,640]{3,2,1,0:T(4,128)(2,1)S(1)} %copy-done.2, f32[2,512,512]{2,1,0:T(8,128)S(1)} %copy-done, f32[2,512,512]{2,1,0:T(8,128)S(1)} %copy-done.1), custom_call_target="tpu_custom_call" | custom-call | tf_op jit(solution)/shard_map/pallas_call | solution.py:323
Async XLA Ops:
  0.6 54.3 %copy-start.3 = (s32[128]{0:T(128)S(1)}, s32[128]{0:T(128)}, u32[]{:S(2)}) copy-start(s32[128]{0:T(128)} %slot_of.1) | copy-start | bytes 1540
  55.0 1.6 %copy-start = (f32[2,512,512]{2,1,0:T(8,128)S(1)}, f32[2,512,512]{2,1,0:T(8,128)}, u32[]{:S(2)}) copy-start(f32[2,512,512]{2,1,0:T(8,128)} %get-tuple-element.7.left) | copy-start | bytes 6291460
  56.5 1.6 %copy-start.1 = (f32[2,512,512]{2,1,0:T(8,128)S(1)}, f32[2,512,512]{2,1,0:T(8,128)}, u32[]{:S(2)}) copy-start(f32[2,512,512]{2,1,0:T(8,128)} %get-tuple-element.8.right) | copy-start | bytes 6291460
  58.1 1.3 %copy-start.2 = (s16[2,128,4,640]{3,2,1,0:T(4,128)(2,1)S(1)}, s16[2,128,4,640]{3,2,1,0:T(4,128)(2,1)}, u32[]{:S(2)}) copy-start(s16[2,128,4,640]{3,2,1,0:T(4,128)(2,1)} %get-tuple-element.6.returned) | copy-start | bytes 3932164

commit v3 on v2

--- a/solution.py
+++ b/solution.py
@@ -273,10 +273,10 @@
         settle(others(returned, j), rr_sem.at[j])
 
 
-def finish(slot_of, returned, left, right, update, new_left, new_right, sems):
+def finish(slot_of, returned, left, right, update_hbm, new_left_hbm, new_right_hbm, update, sems):
     copies = [
-        pltpu.make_async_copy(left, new_left, sems.at[0]),
-        pltpu.make_async_copy(right, new_right, sems.at[1]),
+        pltpu.make_async_copy(left, new_left_hbm, sems.at[0]),
+        pltpu.make_async_copy(right, new_right_hbm, sems.at[1]),
     ]
     for copy in copies:
         copy.start()
@@ -289,20 +289,27 @@
         update[b] = values * jnp.concatenate([scale] * (B // 128), axis=1)
         return carry
 
-    lax.fori_loop(0, NBLK, gather, 0, unroll=8)
+    share = NBLK // 2
+    for part in range(2):
+        lax.fori_loop(part * share, (part + 1) * share, gather, 0, unroll=8)
+        rows = pl.ds(part * share, share)
+        copies.append(pltpu.make_async_copy(update.at[rows], update_hbm.at[rows], sems.at[2 + part]))
+        copies[-1].start()
     for copy in copies:
         copy.wait()
 
 
 def per_device(grads, block_slot, iters_count, stat_left, stat_right):
-    smem, vmem, hbm = (pl.BlockSpec(memory_space=m) for m in (pltpu.SMEM, pltpu.VMEM, pl.ANY))
+    smem, vmem, hbm, free = (
+        pl.BlockSpec(memory_space=m) for m in (pltpu.SMEM, pltpu.VMEM, pltpu.HBM, pl.ANY)
+    )
     dma = pltpu.SemaphoreType.DMA
     stats = jax.ShapeDtypeStruct((CAP, B, B), F32)
     returned, left, right = pl.pallas_call(
         kernel,
         out_shape=(jax.ShapeDtypeStruct((CAP, NDEV, ROWS, WIDE), jnp.int16), stats, stats),
         in_specs=[hbm] * 5,
-        out_specs=(hbm, hbm, hbm),
+        out_specs=(free, free, free),
         scratch_shapes=[pltpu.VMEM((1, NBLK), jnp.int32)] * 2
         + [pltpu.VMEM((NBLK, ROWS, B), BF16)]
         + [pltpu.VMEM((CAP, B, B), F32)] * 4
@@ -317,16 +324,16 @@
         + [pltpu.VMEM((2, B, B), t) for _, t in PAIRS]
         + [pltpu.VMEM((B, B), t) for _, t in SINGLES],
         compiler_params=pltpu.CompilerParams(
-            collective_id=0, has_side_effects=True, vmem_limit_bytes=56 * 2**20
+            collective_id=0, has_side_effects=True, vmem_limit_bytes=48 * 2**20
         ),
     )(block_slot.reshape(1, NBLK), iters_count.reshape(1, NBLK), grads, stat_left, stat_right)
     return pl.pallas_call(
         finish,
         out_shape=(jax.ShapeDtypeStruct((NBLK, ROWS, B), F32), stats, stats),
-        in_specs=[smem, vmem, hbm, hbm],
-        out_specs=(vmem, hbm, hbm),
-        scratch_shapes=[dma((2,))],
-        compiler_params=pltpu.CompilerParams(vmem_limit_bytes=16 * 2**20),
+        in_specs=[smem, vmem, vmem, vmem],
+        out_specs=(hbm, hbm, hbm),
+        scratch_shapes=[pltpu.VMEM((NBLK, ROWS, B), F32), dma((4,))],
+        compiler_params=pltpu.CompilerParams(vmem_limit_bytes=12 * 2**20),
     )(block_slot, returned, left, right)
 
 

time: 63.2 us -> 60.3 us (0.954)
  local copies, waits for them, and re-layouts: 4.49 us -> 2.34 us
  Pallas kernels: 57.8 us -> 57.1 us
    unnamed x8 -> x6, local copies, waits for them, and re-layouts: 4.49 us -> 2.34 us
where the time goes in v3:
time: 60.3 us; the launch traced here: 60.1 us
  Pallas kernels  57.1 us (95%)
  local copies, waits for them, and re-layouts  2.34 us (4%)
  between operations  0.65 us (1%)
    pallas_call x1, Pallas kernels, per_device(): pl.pallas_call(kernel, out_shape=(jax.ShapeDtypeStruct((CAP, NDEV, ROWS,...  54.2 us
    pallas_call x1, Pallas kernels, per_device(): pl.pallas_call(finish, out_shape=(jax.ShapeDtypeStruct((NBLK, ROWS, B), F...  2.91 us
    unnamed x6, local copies, waits for them, and re-layouts  2.34 us

profile of v3, /device:TPU:1, one launch (start us, length us, event | category | flops | bytes accessed | tf_op | source)
XLA Modules:
  0.0 60.1 jit_solution(8812442270414554602)
XLA Ops:
  0.6 0.0 copy-start
  0.6 1.0 %copy-done = bf16[128,4,512]{2,1,0:T(4,128)(2,1)S(1)} copy-done((bf16[128,4,512]{2,1,0:T(4,128)(2,1)S(1)}, bf16[128,4,512]{2,1,0:T(4,128)(2,1)}, u32[]{:S(2)}) %copy-start) | copy-done | bytes 524312
  1.7 0.0 copy-start.1
  1.7 0.7 %copy-done.1 = s32[128]{0:T(128)S(1)} copy-done((s32[128]{0:T(128)S(1)}, s32[128]{0:T(128)}, u32[]{:S(2)}) %copy-start.1) | copy-done | bytes 536
  2.3 0.0 copy-start.2
  2.3 0.7 %copy-done.2 = s32[128]{0:T(128)S(1)} copy-done((s32[128]{0:T(128)S(1)}, s32[128]{0:T(128)}, u32[]{:S(2)}) %copy-start.2) | copy-done | bytes 536
  3.0 54.2 %shard_map.76 = (s16[2,128,4,640]{3,2,1,0:T(4,128)(2,1)S(1)}, f32[2,512,512]{2,1,0:T(8,128)S(1)}, f32[2,512,512]{2,1,0:T(8,128)S(1)}) custom-call(s32[1,128]{1,0:T(1,128)S(1)} %bitcast.2, s32[1,128]{1,0:T(1,128)S(1)} %bitcast.3, bf16[128,4,512]{2,1,0:T(4,128)(2,1)S(1)} %copy-done, f32[2,512,512]{2,1,0:T(8,128)} %left_hbm.1, f32[2,512,512]{2,1,0:T(8,128)} %right_hbm.1), custom_call_target="tpu_custom_call" | custom-call | tf_op jit(solution)/shard_map/pallas_call | solution.py:308
  57.2 2.9 %shard_map.77 = (f32[128,4,512]{2,1,0:T(4,128)}, f32[2,512,512]{2,1,0:T(8,128)}, f32[2,512,512]{2,1,0:T(8,128)}) custom-call(s32[128]{0:T(128)S(1)} %copy-done.1, s16[2,128,4,640]{3,2,1,0:T(4,128)(2,1)S(1)} %get-tuple-element.6.returned, f32[2,512,512]{2,1,0:T(8,128)S(1)} %get-tuple-element.7.left, f32[2,512,512]{2,1,0:T(8,128)S(1)} %get-tuple-element.8.right), custom_call_target="tpu_custom_call" | custom-call | tf_op jit(solution)/shard_map/pallas_call | solution.py:330
Async XLA Ops:
  0.6 1.0 %copy-start = (bf16[128,4,512]{2,1,0:T(4,128)(2,1)S(1)}, bf16[128,4,512]{2,1,0:T(4,128)(2,1)}, u32[]{:S(2)}) copy-start(bf16[128,4,512]{2,1,0:T(4,128)(2,1)} %grads_hbm.1) | copy-start | bytes 1572868
  1.7 0.7 %copy-start.1 = (s32[128]{0:T(128)S(1)}, s32[128]{0:T(128)}, u32[]{:S(2)}) copy-start(s32[128]{0:T(128)} %slot_of.1) | copy-start | bytes 1540
  2.3 0.7 %copy-start.2 = (s32[128]{0:T(128)S(1)}, s32[128]{0:T(128)}, u32[]{:S(2)}) copy-start(s32[128]{0:T(128)} %param.7) | copy-start | bytes 1540

commit v4 on v3

--- a/solution.py
+++ b/solution.py
@@ -56,56 +56,107 @@
     return z * 2 + core, y * 4 + x
 
 
+HALF = B // 2
+LOW, HIGH, ALL = slice(0, HALF), slice(HALF, B), slice(0, B)
+UPPER = ((LOW, ALL), (HIGH, HIGH))
+
+
+def put(ref, top, corner):
+    ref[LOW, :] = top
+    ref[HIGH, HIGH] = corner
+    ref[HIGH, LOW] = jnp.transpose(top[:, HIGH])
+
+
+def put_split(high, low, top, corner):
+    (top_high, top_low), (corner_high, corner_low) = split(top), split(corner)
+    put(high, top_high, corner_high)
+    put(low, top_low, corner_low)
+
+
+def upper(former, latter):
+    return dot(former[LOW, :], latter[...]), dot(former[HIGH, :], latter[:, HIGH])
+
+
+def upper_split(f_high, f_low, l_high, l_low):
+    return tuple(
+        dot(f_high[rows, :], l_high[:, cols])
+        + dot(f_high[rows, :], l_low[:, cols])
+        + dot(f_low[rows, :], l_high[:, cols])
+        for rows, cols in UPPER
+    )
+
+
+def wide(ref, at):
+    return ref[at].astype(F32)
+
+
 def roots_and_product(g, sl, sr, nl, nr, squared, live, three, s):
     fs = []
     for side, (stat, fresh) in enumerate(((sl, nl), (sr, nr))):
-        dims = (((1,), (1,)), ((), ())) if side == 0 else (((0,), (0,)), ((), ()))
-        gram = lax.dot_general(g[...], g[...], dims, preferred_element_type=F32)
-        old = stat[...]
-        a = STAT_DECAY * old + squared * gram
-        a = jnp.where(live, a, old)
-        fresh[...] = a
-        fs.append(1.0 / jnp.sqrt(total(a * a)))
+        sums = []
+        for rows, cols in UPPER:
+            if side == 0:
+                former, latter, over = g[rows, :], g[cols, :], 1
+            else:
+                former, latter, over = g[:, rows], g[:, cols], 0
+            gram = lax.dot_general(former, latter, (((over,), (over,)), ((), ())), preferred_element_type=F32)
+            targets = [((rows, cols), gram)]
+            if rows == LOW:
+                targets.append(((HIGH, LOW), jnp.transpose(gram[:, HIGH])))
+            for at, part in targets:
+                old = stat[at]
+                a = jnp.where(live, STAT_DECAY * old + squared * part, old)
+                fresh[at] = a
+                sums.append(total(a * a))
+        fs.append(1.0 / jnp.sqrt(sums[0] + sums[1] + sums[2]))
     a_of = (nl, nr)
     both = (0, 1)
+    at2 = lambda name, i: s[name].at[i]
     for i in both:
         s["mh"][i], s["ml"][i] = split(a_of[i][...] * fs[i])
     for i in both:
-        square = dot(s["mh"][i], s["mh"][i])
-        s["d"][i] = (a_of[i][...] * (-0.625 * fs[i]) + square * 0.0625).astype(BF16)
-    for i in both:
-        f = s["d"][i].astype(F32) * 3.125 + dot(s["d"][i], s["d"][i])
-        s["fh"][i], s["fl"][i] = split(f)
-    for i in both:
-        n = (
-            a_of[i][...] * (1.25**4 * fs[i])
-            + dot(s["fh"][i], s["mh"][i])
-            + dot(s["fh"][i], s["ml"][i])
-            + dot(s["fl"][i], s["mh"][i])
-        )
-        s["n"][i] = n
-        s["nh"][i], s["nl"][i] = split(n)
-    for i in both:
-        square = dot(s["nh"][i], s["nh"][i]) + dot(s["nh"][i], s["nl"][i]) + dot(s["nl"][i], s["nh"][i])
-        s["s"][i] = square.astype(BF16)
-    for i in both:
-        c = dot(s["s"][i], s["nh"][i])
-        s["c"][i] = c.astype(BF16)
-        s["b"][i] = (V[4] * s["nh"][i].astype(F32) + V[5] * s["s"][i].astype(F32) + V[6] * c).astype(BF16)
+        square = upper(at2("mh", i), at2("mh", i))
+        d = [(a_of[i][at] * (-0.625 * fs[i]) + v * 0.0625).astype(BF16) for at, v in zip(UPPER, square)]
+        put(at2("d", i), *d)
+    for i in both:
+        square = upper(at2("d", i), at2("d", i))
+        f = [wide(at2("d", i), at) * 3.125 + v for at, v in zip(UPPER, square)]
+        put_split(at2("fh", i), at2("fl", i), *f)
+    for i in both:
+        product = upper_split(at2("fh", i), at2("fl", i), at2("mh", i), at2("ml", i))
+        n = [a_of[i][at] * (1.25**4 * fs[i]) + v for at, v in zip(UPPER, product)]
+        for at, v in zip(UPPER, n):
+            at2("n", i)[at] = v
+        put_split(at2("nh", i), at2("nl", i), *n)
+    for i in both:
+        square = upper_split(at2("nh", i), at2("nl", i), at2("nh", i), at2("nl", i))
+        put(at2("s", i), *[v.astype(BF16) for v in square])
+    for i in both:
+        c = upper(at2("s", i), at2("nh", i))
+        put(at2("c", i), *[v.astype(BF16) for v in c])
+        last = [
+            V[4] * wide(at2("nh", i), at) + V[5] * wide(at2("s", i), at) + V[6] * v
+            for at, v in zip(UPPER, c)
+        ]
+        put(at2("b", i), *[v.astype(BF16) for v in last])
     w0, w1 = jnp.where(three, V[0], 1.25), jnp.where(three, V[1], -0.25)
     w2, w3, w4 = jnp.where(three, V[2], 0.0), jnp.where(three, V[3], 0.0), jnp.where(three, 1.0, 0.0)
     for i in both:
-        u = (
-            w1 * s["n"][i]
-            + w2 * s["s"][i].astype(F32)
-            + w3 * s["c"][i].astype(F32)
-            + w4 * dot(s["c"][i], s["b"][i])
-        )
-        s["n"][i] = u
-        s["u"][i] = u.astype(BF16)
-    for i in both:
-        z = 1.25 * s["n"][i] - a_of[i][...] * (fs[i] * w0 * 0.25) - 0.25 * dot(s["mh"][i], s["u"][i])
-        s["zh"][i], s["zl"][i] = split(z)
+        product = upper(at2("c", i), at2("b", i))
+        u = [
+            w1 * at2("n", i)[at] + w2 * wide(at2("s", i), at) + w3 * wide(at2("c", i), at) + w4 * v
+            for at, v in zip(UPPER, product)
+        ]
+        for at, v in zip(UPPER, u):
+            at2("n", i)[at] = v
+        put(at2("u", i), *[v.astype(BF16) for v in u])
+    for i in both:
+        product = upper(at2("mh", i), at2("u", i))
+        z = [
+            1.25 * at2("n", i)[at] - a_of[i][at] * (fs[i] * w0 * 0.25) - 0.25 * v
+            for at, v in zip(UPPER, product)
+        ]
+        put_split(at2("zh", i), at2("zl", i), *z)
     alpha = 1.25 * w0
     h = alpha * g[...].astype(F32) + dot(s["zh"][0], g[...]) + dot(s["zl"][0], g[...])
     s["p"][...] = h

time: 60.3 us -> 56.3 us (0.934)
  Pallas kernels: 57.1 us -> 53.1 us
    pallas_call x1, Pallas kernels: 54.2 us -> 50.2 us  [per_device(): pl.pallas_call(kernel, out_shape=(jax.ShapeDtypeStruct((CAP, NDEV, ROWS,...]
where the time goes in v4:
time: 56.3 us; the launch traced here: 56.1 us
  Pallas kernels  53.1 us (94%)
  local copies, waits for them, and re-layouts  2.34 us (4%)
  between operations  0.65 us (1%)
    pallas_call x1, Pallas kernels, per_device(): pl.pallas_call(kernel, out_shape=(jax.ShapeDtypeStruct((CAP, NDEV, ROWS,...  50.2 us
    pallas_call x1, Pallas kernels, per_device(): pl.pallas_call(finish, out_shape=(jax.ShapeDtypeStruct((NBLK, ROWS, B), F...  2.91 us
    unnamed x6, local copies, waits for them, and re-layouts  2.34 us

profile of v4, /device:TPU:1, one launch (start us, length us, event | category | flops | bytes accessed | tf_op | source)
XLA Modules:
  0.0 56.1 jit_solution(4016210840876877051)
XLA Ops:
  0.6 0.0 copy-start
  0.6 1.0 %copy-done = bf16[128,4,512]{2,1,0:T(4,128)(2,1)S(1)} copy-done((bf16[128,4,512]{2,1,0:T(4,128)(2,1)S(1)}, bf16[128,4,512]{2,1,0:T(4,128)(2,1)}, u32[]{:S(2)}) %copy-start) | copy-done | bytes 524312
  1.7 0.0 copy-start.1
  1.7 0.7 %copy-done.1 = s32[128]{0:T(128)S(1)} copy-done((s32[128]{0:T(128)S(1)}, s32[128]{0:T(128)}, u32[]{:S(2)}) %copy-start.1) | copy-done | bytes 536
  2.3 0.0 copy-start.2
  2.3 0.7 %copy-done.2 = s32[128]{0:T(128)S(1)} copy-done((s32[128]{0:T(128)S(1)}, s32[128]{0:T(128)}, u32[]{:S(2)}) %copy-start.2) | copy-done | bytes 536
  3.0 50.2 %shard_map.76 = (s16[2,128,4,640]{3,2,1,0:T(4,128)(2,1)S(1)}, f32[2,512,512]{2,1,0:T(8,128)S(1)}, f32[2,512,512]{2,1,0:T(8,128)S(1)}) custom-call(s32[1,128]{1,0:T(1,128)S(1)} %bitcast.2, s32[1,128]{1,0:T(1,128)S(1)} %bitcast.3, bf16[128,4,512]{2,1,0:T(4,128)(2,1)S(1)} %copy-done, f32[2,512,512]{2,1,0:T(8,128)} %left_hbm.1, f32[2,512,512]{2,1,0:T(8,128)} %right_hbm.1), custom_call_target="tpu_custom_call" | custom-call | tf_op jit(solution)/shard_map/pallas_call | solution.py:359
  53.2 2.9 %shard_map.77 = (f32[128,4,512]{2,1,0:T(4,128)}, f32[2,512,512]{2,1,0:T(8,128)}, f32[2,512,512]{2,1,0:T(8,128)}) custom-call(s32[128]{0:T(128)S(1)} %copy-done.1, s16[2,128,4,640]{3,2,1,0:T(4,128)(2,1)S(1)} %get-tuple-element.6.returned, f32[2,512,512]{2,1,0:T(8,128)S(1)} %get-tuple-element.7.left, f32[2,512,512]{2,1,0:T(8,128)S(1)} %get-tuple-element.8.right), custom_call_target="tpu_custom_call" | custom-call | tf_op jit(solution)/shard_map/pallas_call | solution.py:381
Async XLA Ops:
  0.6 1.0 %copy-start = (bf16[128,4,512]{2,1,0:T(4,128)(2,1)S(1)}, bf16[128,4,512]{2,1,0:T(4,128)(2,1)}, u32[]{:S(2)}) copy-start(bf16[128,4,512]{2,1,0:T(4,128)(2,1)} %grads_hbm.1) | copy-start | bytes 1572868
  1.7 0.7 %copy-start.1 = (s32[128]{0:T(128)S(1)}, s32[128]{0:T(128)}, u32[]{:S(2)}) copy-start(s32[128]{0:T(128)} %slot_of.1) | copy-start | bytes 1540
  2.3 0.7 %copy-start.2 = (s32[128]{0:T(128)S(1)}, s32[128]{0:T(128)}, u32[]{:S(2)}) copy-start(s32[128]{0:T(128)} %param.7) | copy-start | bytes 1540

commit v5 on v4

--- a/solution.py
+++ b/solution.py
@@ -18,9 +18,8 @@
 DP = 8
 MP = 16
 ROWS = B // NDEV
-WIDE = B + 128
-LEVELS = 32766.0
-STEPS = 64.0
+OCTAVES = 18
+LEVELS = 32760.0 / OCTAVES
 UNROLL = 127
 
 BF16 = jnp.bfloat16
@@ -180,8 +179,8 @@
 
 
 def kernel(
-    slot_hbm, counts_hbm, grads_hbm, left_hbm, right_hbm, returned, new_left_hbm, new_right_hbm,
-    slot_of, counts, grads, left, right, new_left, new_right, fsend, frecv, rsend, psend, precv, gsend, grecv, plan_v, plan,
+    tables_hbm, grads_hbm, left_hbm, right_hbm, returned, new_left_hbm, new_right_hbm, unit_out,
+    tables, grads, left, right, new_left, new_right, fsend, frecv, rsend, psend, precv, gsend, grecv, plan_v, plan,
     local_sem, out_sem, fs_sem, fr_sem, rs_sem, rr_sem, ps_sem, pr_sem, round_sem, *rest,
 ):
     s = dict(zip(NAMES, rest, strict=True))
@@ -194,27 +193,23 @@
     for k in range(1, MP):
         pl.semaphore_signal(barrier, inc=1, device_id=(dp, (mp + k) & (MP - 1)), device_id_type=MESH)
 
-    tables = [
-        pltpu.make_async_copy(slot_hbm, slot_of, local_sem.at[2]),
-        pltpu.make_async_copy(counts_hbm, counts, local_sem.at[3]),
-    ]
-    rows = pltpu.make_async_copy(grads_hbm, grads, local_sem.at[4])
+    names = pltpu.make_async_copy(tables_hbm, tables, local_sem.at[2])
+    rows = pltpu.make_async_copy(grads_hbm, grads, local_sem.at[3])
     loads = [
         pltpu.make_async_copy(left_hbm, left, local_sem.at[0]),
         pltpu.make_async_copy(right_hbm, right, local_sem.at[1]),
     ]
-    for load in [*tables, rows, *loads]:
+    for load in [names, rows, *loads]:
         load.start()
-    for load in tables:
-        load.wait()
+    names.wait()
 
     lane = lax.broadcasted_iota(jnp.int32, (NBLK, NBLK), 1)
-    marks = jnp.transpose(lane * 4 + jnp.broadcast_to(counts[...] & 3, (NBLK, NBLK)))
-    named = jnp.transpose(jnp.broadcast_to(slot_of[...], (NBLK, NBLK)))
+    marks = jnp.transpose(lane * 4 + jnp.broadcast_to(tables[1:2, :] & 3, (NBLK, NBLK)))
+    named = jnp.transpose(jnp.broadcast_to(tables[0:1, :], (NBLK, NBLK)))
     for half in range(CAP):
         found = jnp.where(named == lane + half * NBLK, marks, 0)
         plan_v[pl.ds(half, 1), :] = jnp.max(found, axis=0, keepdims=True)
-    to_scalars = pltpu.make_async_copy(plan_v, plan, local_sem.at[5])
+    to_scalars = pltpu.make_async_copy(plan_v, plan, local_sem.at[4])
     to_scalars.start()
 
     rows.wait()
@@ -286,10 +281,11 @@
         s["g"][...] = arrived
         wide = arrived.astype(F32)
         grad_square = total(wide * wide)
-        square_sum = total(jnp.sum(grecv[...], axis=0))
-        clipping = jnp.minimum(
-            1.0, CLIP_SHARE * B * math.sqrt(NBLK) / (jnp.sqrt(square_sum) + EPSILON)
-        )
+        norm = jnp.sqrt(total(jnp.sum(grecv[...], axis=0)))
+        clipping = jnp.minimum(1.0, CLIP_SHARE * B * math.sqrt(NBLK) / (norm + EPSILON))
+        bound = clipping * norm * (4.0 * norm / (4.0 * norm + EPSILON))
+        unit = jnp.maximum(bound * 2.0**-OCTAVES, 1e-30)
+        unit_out[...] = jnp.broadcast_to(unit, (8, 128))
         my_slot = me * CAP + j
         granted = plan[my_slot >> 7, my_slot & (NBLK - 1)] & 3
         prod_square = roots_and_product(
@@ -299,13 +295,10 @@
         pltpu.make_async_copy(new_left.at[j], new_left_hbm.at[j], out_sem.at[0, j]).start()
         pltpu.make_async_copy(new_right.at[j], new_right_hbm.at[j], out_sem.at[1, j]).start()
         graft = clipping * jnp.sqrt(grad_square) / (jnp.sqrt(prod_square) + EPSILON)
-        scaled = s["p"][...] * graft
-        largest = jnp.maximum(jnp.max(jnp.abs(scaled), axis=1, keepdims=True), 1e-30)
-        code = jnp.ceil(jnp.log2(largest * (1.0 / LEVELS)) * STEPS)
-        levels = jnp.round(scaled * jnp.exp2(code * (-1.0 / STEPS)))
-        rsend[j, :, :, 0:B] = levels.astype(jnp.int32).astype(jnp.int16).reshape(NDEV, ROWS, B)
-        codes = jnp.broadcast_to(code.astype(jnp.int32), (B, 128)).astype(jnp.int16)
-        rsend[j, :, :, B:WIDE] = codes.reshape(NDEV, ROWS, 128)
+        product = s["p"][...]
+        level = jnp.round(jnp.log2(1.0 + jnp.abs(product) * (graft / unit)) * LEVELS)
+        level = jnp.where(product < 0.0, -level, level).astype(jnp.int32).astype(jnp.int16)
+        rsend[j] = level.reshape(NDEV, ROWS, B)
         exchange(rsend, returned, j, rs_sem, rr_sem)
         pltpu.make_async_copy(rsend.at[j, me], returned.at[j, me], out_sem.at[2, j]).start()
         return carry
@@ -324,7 +317,7 @@
         settle(others(returned, j), rr_sem.at[j])
 
 
-def finish(slot_of, returned, left, right, update_hbm, new_left_hbm, new_right_hbm, update, sems):
+def finish(slot_of, returned, left, right, unit, update_hbm, new_left_hbm, new_right_hbm, update, sems):
     copies = [
         pltpu.make_async_copy(left, new_left_hbm, sems.at[0]),
         pltpu.make_async_copy(right, new_right_hbm, sems.at[1]),
@@ -335,9 +328,9 @@
     def gather(b, carry):
         at = slot_of[b]
         piece = returned[at & 1, at >> 1]
-        scale = jnp.exp2(piece[:, B:WIDE].astype(jnp.int32).astype(F32) * (1.0 / STEPS))
-        values = piece[:, 0:B].astype(jnp.int32).astype(F32)
-        update[b] = values * jnp.concatenate([scale] * (B // 128), axis=1)
+        level = piece.astype(jnp.int32).astype(F32)
+        size = (jnp.exp2(jnp.abs(level) * (1.0 / LEVELS)) - 1.0) * unit[0:1, 0:1]
+        update[b] = jnp.where(level < 0.0, -size, size)
         return carry
 
     share = NBLK // 2
@@ -356,20 +349,20 @@
     )
     dma = pltpu.SemaphoreType.DMA
     stats = jax.ShapeDtypeStruct((CAP, B, B), F32)
-    returned, left, right = pl.pallas_call(
+    returned, left, right, unit = pl.pallas_call(
         kernel,
-        out_shape=(jax.ShapeDtypeStruct((CAP, NDEV, ROWS, WIDE), jnp.int16), stats, stats),
-        in_specs=[hbm] * 5,
-        out_specs=(free, free, free),
-        scratch_shapes=[pltpu.VMEM((1, NBLK), jnp.int32)] * 2
+        out_shape=(jax.ShapeDtypeStruct((CAP, NDEV, ROWS, B), jnp.int16), stats, stats, jax.ShapeDtypeStruct((8, 128), F32)),
+        in_specs=[hbm] * 4,
+        out_specs=(free, free, free, vmem),
+        scratch_shapes=[pltpu.VMEM((2, NBLK), jnp.int32)]
         + [pltpu.VMEM((NBLK, ROWS, B), BF16)]
         + [pltpu.VMEM((CAP, B, B), F32)] * 4
         + [pltpu.VMEM((CAP, NDEV, ROWS, B), BF16)] * 2
-        + [pltpu.VMEM((CAP, NDEV, ROWS, WIDE), jnp.int16)]
+        + [pltpu.VMEM((CAP, NDEV, ROWS, B), jnp.int16)]
         + [pltpu.VMEM((ROWS, 128), F32), pltpu.VMEM((DP, ROWS, 128), F32)]
         + [pltpu.VMEM((ROWS, 128), F32), pltpu.VMEM((MP, ROWS, 128), F32)]
         + [pltpu.VMEM((CAP, NBLK), jnp.int32), pltpu.SMEM((CAP, NBLK), jnp.int32)]
-        + [dma((6,)), dma((3, CAP))]
+        + [dma((5,)), dma((3, CAP))]
         + [dma((CAP,))] * 6
         + [pltpu.SemaphoreType.REGULAR]
         + [pltpu.VMEM((2, B, B), t) for _, t in PAIRS]
@@ -377,15 +370,15 @@
         compiler_params=pltpu.CompilerParams(
             collective_id=0, has_side_effects=True, vmem_limit_bytes=48 * 2**20
         ),
-    )(block_slot.reshape(1, NBLK), iters_count.reshape(1, NBLK), grads, stat_left, stat_right)
+    )(jnp.stack([block_slot, iters_count]), grads, stat_left, stat_right)
     return pl.pallas_call(
         finish,
         out_shape=(jax.ShapeDtypeStruct((NBLK, ROWS, B), F32), stats, stats),
-        in_specs=[smem, vmem, vmem, vmem],
+        in_specs=[smem, vmem, vmem, vmem, vmem],
         out_specs=(hbm, hbm, hbm),
         scratch_shapes=[pltpu.VMEM((NBLK, ROWS, B), F32), dma((4,))],
         compiler_params=pltpu.CompilerParams(vmem_limit_bytes=12 * 2**20),
-    )(block_slot, returned, left, right)
+    )(block_slot, returned, left, right, unit)
 
 
 def solution(mesh):

time: 56.3 us -> 54.6 us (0.970)
  local copies, waits for them, and re-layouts: 2.34 us -> 1.04 us
  Pallas kernels: 53.1 us -> 52 us
  other arithmetic: 0 us -> 0.68 us
    unnamed x6 -> x4, local copies, waits for them, and re-layouts: 2.34 us -> 1.04 us
    pallas_call x1, Pallas kernels: 50.2 us -> 49.1 us  [per_device(): pl.pallas_call(kernel, out_shape=(jax.ShapeDtypeStruct((CAP, NDEV, ROWS,...]
    another operation x0 -> x1, other arithmetic: none -> 0.68 us  [per_device(): jnp.stack([block_slot, iters_count])]
where the time goes in v5:
time: 54.6 us; the launch traced here: 54.4 us
  Pallas kernels  52 us (95%)
  local copies, waits for them, and re-layouts  1.04 us (2%)
  other arithmetic  0.68 us (1%)
  between operations  0.65 us (1%)
    pallas_call x1, Pallas kernels, per_device(): pl.pallas_call(kernel, out_shape=(jax.ShapeDtypeStruct((CAP, NDEV, ROWS,...  49.1 us
    pallas_call x1, Pallas kernels, per_device(): pl.pallas_call(finish, out_shape=(jax.ShapeDtypeStruct((NBLK, ROWS, B), F...  2.91 us

profile of v5, /device:TPU:1, one launch (start us, length us, event | category | flops | bytes accessed | tf_op | source)
XLA Modules:
  0.0 54.4 jit_solution(15005506117949362244)
XLA Ops:
  0.6 0.7 %pad_add_fusion.tables_hbm = s32[2,128]{1,0:T(2,128)S(1)} fusion(s32[1,128]{1,0:T(1,128)} %bitcast.3, s32[1,128]{1,0:T(1,128)} %bitcast.2), kind=kLoop, calls=%fused_computation | loop fusion | flops 256 | bytes 2048 | tf_op jit(solution)/shard_map/stack | solution.py:373
  1.3 0.0 copy-start
  1.3 1.0 %copy-done = bf16[128,4,512]{2,1,0:T(4,128)(2,1)S(1)} copy-done((bf16[128,4,512]{2,1,0:T(4,128)(2,1)S(1)}, bf16[128,4,512]{2,1,0:T(4,128)(2,1)}, u32[]{:S(2)}) %copy-start) | copy-done | bytes 524312
  2.4 0.0 copy-start.1
  2.4 49.1 %shard_map.76 = (s16[2,128,4,512]{3,2,1,0:T(4,128)(2,1)S(1)}, f32[2,512,512]{2,1,0:T(8,128)S(1)}, f32[2,512,512]{2,1,0:T(8,128)S(1)}, f32[8,128]{1,0:T(8,128)S(1)}) custom-call(s32[2,128]{1,0:T(2,128)S(1)} %pad_add_fusion.tables_hbm, bf16[128,4,512]{2,1,0:T(4,128)(2,1)S(1)} %copy-done, f32[2,512,512]{2,1,0:T(8,128)} %left_hbm.1, f32[2,512,512]{2,1,0:T(8,128)} %right_hbm.1), custom_call_target="tpu_custom_call" | custom-call | tf_op jit(solution)/shard_map/pallas_call | solution.py:352
  51.5 0.0 copy-done.1
  51.5 2.9 %shard_map.77 = (f32[128,4,512]{2,1,0:T(4,128)}, f32[2,512,512]{2,1,0:T(8,128)}, f32[2,512,512]{2,1,0:T(8,128)}) custom-call(s32[128]{0:T(128)S(1)} %copy-done.1, s16[2,128,4,512]{3,2,1,0:T(4,128)(2,1)S(1)} %get-tuple-element.7.returned, f32[2,512,512]{2,1,0:T(8,128)S(1)} %get-tuple-element.8.left, f32[2,512,512]{2,1,0:T(8,128)S(1)} %get-tuple-element.9.right, ...), custom_call_target="tpu_custom_call" | custom-call | tf_op jit(solution)/shard_map/pallas_call | solution.py:374
Async XLA Ops:
  1.3 1.0 %copy-start = (bf16[128,4,512]{2,1,0:T(4,128)(2,1)S(1)}, bf16[128,4,512]{2,1,0:T(4,128)(2,1)}, u32[]{:S(2)}) copy-start(bf16[128,4,512]{2,1,0:T(4,128)(2,1)} %grads_hbm.1) | copy-start | bytes 1572868
  2.4 49.1 %copy-start.1 = (s32[128]{0:T(128)S(1)}, s32[128]{0:T(128)}, u32[]{:S(2)}) copy-start(s32[128]{0:T(128)} %slot_of.1) | copy-start | bytes 1540

commit v6 on v5

--- a/solution.py
+++ b/solution.py
@@ -180,7 +180,7 @@
 
 def kernel(
     tables_hbm, grads_hbm, left_hbm, right_hbm, returned, new_left_hbm, new_right_hbm, unit_out,
-    tables, grads, left, right, new_left, new_right, fsend, frecv, rsend, psend, precv, gsend, grecv, plan_v, plan,
+    tables, grads, left, right, new_left, new_right, fsend, frecv, rsend, psend, precv, gsend, grecv, plan_v, plan, unit_v,
     local_sem, out_sem, fs_sem, fr_sem, rs_sem, rr_sem, ps_sem, pr_sem, round_sem, *rest,
 ):
     s = dict(zip(NAMES, rest, strict=True))
@@ -275,17 +275,20 @@
         load.wait()
     settle(grecv.at[pl.ds(0, MP - 1)], pr_sem.at[1])
 
+    norm = jnp.sqrt(total(jnp.sum(grecv[...], axis=0)))
+    clipping = jnp.minimum(1.0, CLIP_SHARE * B * math.sqrt(NBLK) / (norm + EPSILON))
+    bound = clipping * norm * (4.0 * norm / (4.0 * norm + EPSILON))
+    unit = jnp.maximum(bound * 2.0**-OCTAVES, 1e-30)
+    unit_v[...] = jnp.broadcast_to(unit, (8, 128))
+    unit_copy = pltpu.make_async_copy(unit_v, unit_out, local_sem.at[5])
+    unit_copy.start()
+
     def slot(j, carry):
         settle(others(frecv, j), fr_sem.at[j])
         arrived = frecv[j].reshape(B, B)
         s["g"][...] = arrived
         wide = arrived.astype(F32)
         grad_square = total(wide * wide)
-        norm = jnp.sqrt(total(jnp.sum(grecv[...], axis=0)))
-        clipping = jnp.minimum(1.0, CLIP_SHARE * B * math.sqrt(NBLK) / (norm + EPSILON))
-        bound = clipping * norm * (4.0 * norm / (4.0 * norm + EPSILON))
-        unit = jnp.maximum(bound * 2.0**-OCTAVES, 1e-30)
-        unit_out[...] = jnp.broadcast_to(unit, (8, 128))
         my_slot = me * CAP + j
         granted = plan[my_slot >> 7, my_slot & (NBLK - 1)] & 3
         prod_square = roots_and_product(
@@ -304,6 +307,7 @@
         return carry
 
     lax.fori_loop(0, CAP, slot, 0)
+    unit_copy.wait()
 
     for j in range(CAP):
         pltpu.make_async_copy(new_left.at[j], new_left_hbm.at[j], out_sem.at[0, j]).wait()
@@ -318,10 +322,12 @@
 
 
 def finish(slot_of, returned, left, right, unit, update_hbm, new_left_hbm, new_right_hbm, update, sems):
-    copies = [
-        pltpu.make_async_copy(left, new_left_hbm, sems.at[0]),
-        pltpu.make_async_copy(right, new_right_hbm, sems.at[1]),
-    ]
+    copies = []
+    for held, out in ((left, new_left_hbm), (right, new_right_hbm)):
+        for j in range(CAP):
+            for rows in (pl.ds(0, HALF), pl.ds(HALF, HALF)):
+                sem = sems.at[len(copies)]
+                copies.append(pltpu.make_async_copy(held.at[j, rows], out.at[j, rows], sem))
     for copy in copies:
         copy.start()
 
@@ -337,7 +343,7 @@
     for part in range(2):
         lax.fori_loop(part * share, (part + 1) * share, gather, 0, unroll=8)
         rows = pl.ds(part * share, share)
-        copies.append(pltpu.make_async_copy(update.at[rows], update_hbm.at[rows], sems.at[2 + part]))
+        copies.append(pltpu.make_async_copy(update.at[rows], update_hbm.at[rows], sems.at[8 + part]))
         copies[-1].start()
     for copy in copies:
         copy.wait()
@@ -353,7 +359,7 @@
         kernel,
         out_shape=(jax.ShapeDtypeStruct((CAP, NDEV, ROWS, B), jnp.int16), stats, stats, jax.ShapeDtypeStruct((8, 128), F32)),
         in_specs=[hbm] * 4,
-        out_specs=(free, free, free, vmem),
+        out_specs=(free, free, free, free),
         scratch_shapes=[pltpu.VMEM((2, NBLK), jnp.int32)]
         + [pltpu.VMEM((NBLK, ROWS, B), BF16)]
         + [pltpu.VMEM((CAP, B, B), F32)] * 4
@@ -361,8 +367,8 @@
         + [pltpu.VMEM((CAP, NDEV, ROWS, B), jnp.int16)]
         + [pltpu.VMEM((ROWS, 128), F32), pltpu.VMEM((DP, ROWS, 128), F32)]
         + [pltpu.VMEM((ROWS, 128), F32), pltpu.VMEM((MP, ROWS, 128), F32)]
-        + [pltpu.VMEM((CAP, NBLK), jnp.int32), pltpu.SMEM((CAP, NBLK), jnp.int32)]
-        + [dma((5,)), dma((3, CAP))]
+        + [pltpu.VMEM((CAP, NBLK), jnp.int32), pltpu.SMEM((CAP, NBLK), jnp.int32), pltpu.VMEM((8, 128), F32)]
+        + [dma((6,)), dma((3, CAP))]
         + [dma((CAP,))] * 6
         + [pltpu.SemaphoreType.REGULAR]
         + [pltpu.VMEM((2, B, B), t) for _, t in PAIRS]
@@ -376,7 +382,7 @@
         out_shape=(jax.ShapeDtypeStruct((NBLK, ROWS, B), F32), stats, stats),
         in_specs=[smem, vmem, vmem, vmem, vmem],
         out_specs=(hbm, hbm, hbm),
-        scratch_shapes=[pltpu.VMEM((NBLK, ROWS, B), F32), dma((4,))],
+        scratch_shapes=[pltpu.VMEM((NBLK, ROWS, B), F32), dma((10,))],
         compiler_params=pltpu.CompilerParams(vmem_limit_bytes=12 * 2**20),
     )(block_slot, returned, left, right, unit)
 

time: 54.6 us -> 54.6 us (level)
  no operation moved by 1% of the time
where the time goes in v6:
time: 54.6 us; the launch traced here: 54.5 us
  Pallas kernels  52.1 us (95%)
  local copies, waits for them, and re-layouts  1.04 us (2%)
  other arithmetic  0.68 us (1%)
  between operations  0.65 us (1%)
    pallas_call x1, Pallas kernels, per_device(): pl.pallas_call(kernel, out_shape=(jax.ShapeDtypeStruct((CAP, NDEV, ROWS,...  49.1 us
    pallas_call x1, Pallas kernels, per_device(): pl.pallas_call(finish, out_shape=(jax.ShapeDtypeStruct((NBLK, ROWS, B), F...  2.96 us

profile of v6, /device:TPU:1, one launch (start us, length us, event | category | flops | bytes accessed | tf_op | source)
XLA Modules:
  0.0 54.5 jit_solution(9380090599174641406)
XLA Ops:
  0.6 0.7 %pad_add_fusion.tables_hbm = s32[2,128]{1,0:T(2,128)S(1)} fusion(s32[1,128]{1,0:T(1,128)} %bitcast.3, s32[1,128]{1,0:T(1,128)} %bitcast.2), kind=kLoop, calls=%fused_computation | loop fusion | flops 256 | bytes 2048 | tf_op jit(solution)/shard_map/stack | solution.py:379
  1.3 0.0 copy-start
  1.3 1.0 %copy-done = bf16[128,4,512]{2,1,0:T(4,128)(2,1)S(1)} copy-done((bf16[128,4,512]{2,1,0:T(4,128)(2,1)S(1)}, bf16[128,4,512]{2,1,0:T(4,128)(2,1)}, u32[]{:S(2)}) %copy-start) | copy-done | bytes 524312
  2.4 0.0 copy-start.1
  2.4 49.1 %shard_map.76 = (s16[2,128,4,512]{3,2,1,0:T(4,128)(2,1)S(1)}, f32[2,512,512]{2,1,0:T(8,128)S(1)}, f32[2,512,512]{2,1,0:T(8,128)S(1)}, f32[8,128]{1,0:T(8,128)S(1)}) custom-call(s32[2,128]{1,0:T(2,128)S(1)} %pad_add_fusion.tables_hbm, bf16[128,4,512]{2,1,0:T(4,128)(2,1)S(1)} %copy-done, f32[2,512,512]{2,1,0:T(8,128)} %left_hbm.1, f32[2,512,512]{2,1,0:T(8,128)} %right_hbm.1), custom_call_target="tpu_custom_call" | custom-call | tf_op jit(solution)/shard_map/pallas_call | solution.py:358
  51.5 0.0 copy-done.1
  51.5 3.0 %shard_map.77 = (f32[128,4,512]{2,1,0:T(4,128)}, f32[2,512,512]{2,1,0:T(8,128)}, f32[2,512,512]{2,1,0:T(8,128)}) custom-call(s32[128]{0:T(128)S(1)} %copy-done.1, s16[2,128,4,512]{3,2,1,0:T(4,128)(2,1)S(1)} %get-tuple-element.7.returned, f32[2,512,512]{2,1,0:T(8,128)S(1)} %get-tuple-element.8.left, f32[2,512,512]{2,1,0:T(8,128)S(1)} %get-tuple-element.9.right, ...), custom_call_target="tpu_custom_call" | custom-call | tf_op jit(solution)/shard_map/pallas_call | solution.py:380
Async XLA Ops:
  1.3 1.0 %copy-start = (bf16[128,4,512]{2,1,0:T(4,128)(2,1)S(1)}, bf16[128,4,512]{2,1,0:T(4,128)(2,1)}, u32[]{:S(2)}) copy-start(bf16[128,4,512]{2,1,0:T(4,128)(2,1)} %grads_hbm.1) | copy-start | bytes 1572868
  2.4 49.1 %copy-start.1 = (s32[128]{0:T(128)S(1)}, s32[128]{0:T(128)}, u32[]{:S(2)}) copy-start(s32[128]{0:T(128)} %slot_of.1) | copy-start | bytes 1540

commit v7 on v5

--- a/solution.py
+++ b/solution.py
@@ -47,7 +47,7 @@
 
 def partner(step):
     dp, mp = lax.axis_index("dp"), lax.axis_index("mp")
-    offset = (step * 59) & (NDEV - 1)
+    offset = (step * 37) & (NDEV - 1)
     core = (dp + offset) & 1
     z = ((dp >> 1) + (offset >> 1)) & 3
     y = ((mp >> 2) + (offset >> 3)) & 3

time: 54.6 us -> 54.2 us (level)
  no operation moved by 1% of the time
where the time goes in v7:
time: 54.2 us; the launch traced here: 54.1 us
  Pallas kernels  51.7 us (95%)
  local copies, waits for them, and re-layouts  1.04 us (2%)
  other arithmetic  0.68 us (1%)
  between operations  0.65 us (1%)
    pallas_call x1, Pallas kernels, per_device(): pl.pallas_call(kernel, out_shape=(jax.ShapeDtypeStruct((CAP, NDEV, ROWS,...  48.8 us
    pallas_call x1, Pallas kernels, per_device(): pl.pallas_call(finish, out_shape=(jax.ShapeDtypeStruct((NBLK, ROWS, B), F...  2.91 us

profile of v7, /device:TPU:1, one launch (start us, length us, event | category | flops | bytes accessed | tf_op | source)
XLA Modules:
  0.0 54.1 jit_solution(10125188870466147715)
XLA Ops:
  0.6 0.7 %pad_add_fusion.tables_hbm = s32[2,128]{1,0:T(2,128)S(1)} fusion(s32[1,128]{1,0:T(1,128)} %bitcast.3, s32[1,128]{1,0:T(1,128)} %bitcast.2), kind=kLoop, calls=%fused_computation | loop fusion | flops 256 | bytes 2048 | tf_op jit(solution)/shard_map/stack | solution.py:373
  1.3 0.0 copy-start
  1.3 1.0 %copy-done = bf16[128,4,512]{2,1,0:T(4,128)(2,1)S(1)} copy-done((bf16[128,4,512]{2,1,0:T(4,128)(2,1)S(1)}, bf16[128,4,512]{2,1,0:T(4,128)(2,1)}, u32[]{:S(2)}) %copy-start) | copy-done | bytes 524312
  2.4 0.0 copy-start.1
  2.4 48.8 %shard_map.76 = (s16[2,128,4,512]{3,2,1,0:T(4,128)(2,1)S(1)}, f32[2,512,512]{2,1,0:T(8,128)S(1)}, f32[2,512,512]{2,1,0:T(8,128)S(1)}, f32[8,128]{1,0:T(8,128)S(1)}) custom-call(s32[2,128]{1,0:T(2,128)S(1)} %pad_add_fusion.tables_hbm, bf16[128,4,512]{2,1,0:T(4,128)(2,1)S(1)} %copy-done, f32[2,512,512]{2,1,0:T(8,128)} %left_hbm.1, f32[2,512,512]{2,1,0:T(8,128)} %right_hbm.1), custom_call_target="tpu_custom_call" | custom-call | tf_op jit(solution)/shard_map/pallas_call | solution.py:352
  51.1 0.0 copy-done.1
  51.1 2.9 %shard_map.77 = (f32[128,4,512]{2,1,0:T(4,128)}, f32[2,512,512]{2,1,0:T(8,128)}, f32[2,512,512]{2,1,0:T(8,128)}) custom-call(s32[128]{0:T(128)S(1)} %copy-done.1, s16[2,128,4,512]{3,2,1,0:T(4,128)(2,1)S(1)} %get-tuple-element.7.returned, f32[2,512,512]{2,1,0:T(8,128)S(1)} %get-tuple-element.8.left, f32[2,512,512]{2,1,0:T(8,128)S(1)} %get-tuple-element.9.right, ...), custom_call_target="tpu_custom_call" | custom-call | tf_op jit(solution)/shard_map/pallas_call | solution.py:374
Async XLA Ops:
  1.3 1.0 %copy-start = (bf16[128,4,512]{2,1,0:T(4,128)(2,1)S(1)}, bf16[128,4,512]{2,1,0:T(4,128)(2,1)}, u32[]{:S(2)}) copy-start(bf16[128,4,512]{2,1,0:T(4,128)(2,1)} %grads_hbm.1) | copy-start | bytes 1572868
  2.4 48.8 %copy-start.1 = (s32[128]{0:T(128)S(1)}, s32[128]{0:T(128)}, u32[]{:S(2)}) copy-start(s32[128]{0:T(128)} %slot_of.1) | copy-start | bytes 1540

commit v8 on v7

--- a/solution.py
+++ b/solution.py
@@ -47,7 +47,7 @@
 
 def partner(step):
     dp, mp = lax.axis_index("dp"), lax.axis_index("mp")
-    offset = (step * 37) & (NDEV - 1)
+    offset = (step * 91) & (NDEV - 1)
     core = (dp + offset) & 1
     z = ((dp >> 1) + (offset >> 1)) & 3
     y = ((mp >> 2) + (offset >> 3)) & 3

time: 54.2 us -> 54.3 us (level)
  no operation moved by 1% of the time
where the time goes in v8:
time: 54.3 us; the launch traced here: 54.1 us
  Pallas kernels  51.8 us (95%)
  local copies, waits for them, and re-layouts  1.04 us (2%)
  other arithmetic  0.68 us (1%)
  between operations  0.65 us (1%)
    pallas_call x1, Pallas kernels, per_device(): pl.pallas_call(kernel, out_shape=(jax.ShapeDtypeStruct((CAP, NDEV, ROWS,...  48.8 us
    pallas_call x1, Pallas kernels, per_device(): pl.pallas_call(finish, out_shape=(jax.ShapeDtypeStruct((NBLK, ROWS, B), F...  2.91 us

profile of v8, /device:TPU:1, one launch (start us, length us, event | category | flops | bytes accessed | tf_op | source)
XLA Modules:
  0.0 54.1 jit_solution(12022263453075714451)
XLA Ops:
  0.6 0.7 %pad_add_fusion.tables_hbm = s32[2,128]{1,0:T(2,128)S(1)} fusion(s32[1,128]{1,0:T(1,128)} %bitcast.3, s32[1,128]{1,0:T(1,128)} %bitcast.2), kind=kLoop, calls=%fused_computation | loop fusion | flops 256 | bytes 2048 | tf_op jit(solution)/shard_map/stack | solution.py:373
  1.3 0.0 copy-start
  1.3 1.0 %copy-done = bf16[128,4,512]{2,1,0:T(4,128)(2,1)S(1)} copy-done((bf16[128,4,512]{2,1,0:T(4,128)(2,1)S(1)}, bf16[128,4,512]{2,1,0:T(4,128)(2,1)}, u32[]{:S(2)}) %copy-start) | copy-done | bytes 524312
  2.4 0.0 copy-start.1
  2.4 48.8 %shard_map.76 = (s16[2,128,4,512]{3,2,1,0:T(4,128)(2,1)S(1)}, f32[2,512,512]{2,1,0:T(8,128)S(1)}, f32[2,512,512]{2,1,0:T(8,128)S(1)}, f32[8,128]{1,0:T(8,128)S(1)}) custom-call(s32[2,128]{1,0:T(2,128)S(1)} %pad_add_fusion.tables_hbm, bf16[128,4,512]{2,1,0:T(4,128)(2,1)S(1)} %copy-done, f32[2,512,512]{2,1,0:T(8,128)} %left_hbm.1, f32[2,512,512]{2,1,0:T(8,128)} %right_hbm.1), custom_call_target="tpu_custom_call" | custom-call | tf_op jit(solution)/shard_map/pallas_call | solution.py:352
  51.2 0.0 copy-done.1
  51.2 2.9 %shard_map.77 = (f32[128,4,512]{2,1,0:T(4,128)}, f32[2,512,512]{2,1,0:T(8,128)}, f32[2,512,512]{2,1,0:T(8,128)}) custom-call(s32[128]{0:T(128)S(1)} %copy-done.1, s16[2,128,4,512]{3,2,1,0:T(4,128)(2,1)S(1)} %get-tuple-element.7.returned, f32[2,512,512]{2,1,0:T(8,128)S(1)} %get-tuple-element.8.left, f32[2,512,512]{2,1,0:T(8,128)S(1)} %get-tuple-element.9.right, ...), custom_call_target="tpu_custom_call" | custom-call | tf_op jit(solution)/shard_map/pallas_call | solution.py:374
Async XLA Ops:
  1.3 1.0 %copy-start = (bf16[128,4,512]{2,1,0:T(4,128)(2,1)S(1)}, bf16[128,4,512]{2,1,0:T(4,128)(2,1)}, u32[]{:S(2)}) copy-start(bf16[128,4,512]{2,1,0:T(4,128)(2,1)} %grads_hbm.1) | copy-start | bytes 1572868
  2.4 48.9 %copy-start.1 = (s32[128]{0:T(128)S(1)}, s32[128]{0:T(128)}, u32[]{:S(2)}) copy-start(s32[128]{0:T(128)} %slot_of.1) | copy-start | bytes 1540
